TPU v7x, 32 devices: a whole 2x2x4 slice. The times are simulated.
32 devices in a mesh: branch: 8 (over z, x), sub: 4 (over y, core).
Axes of the slice: x: 2, y: 2, z: 4, core: 2. Of those that a mesh axis runs over, the one named last changes fastest.
Arguments:
- vectors: float32 [1152, 16, 128], P(('branch', 'sub')), may hold values from -6 to 6
- leaf_basis: float32 [1152, 64, 128], P(('branch', 'sub')), may hold values from -0.5 to 0.5
- near_index: int32 [1152, 3], P(('branch', 'sub')), may hold values from 0 to 1151, as said below
- near_blocks: float32 [1152, 3, 128, 128], P(('branch', 'sub')), may hold values from -0.3125 to 0.3125
- coupling_index: int32 [1152, 4], P(('branch', 'sub')), may hold values from 0 to 1151, as said below
- coupling_blocks: float32 [1152, 4, 64, 64], P(('branch', 'sub')), may hold values from -0.375 to 0.375
- leaf_transfer: float32 [1152, 64, 64], P(('branch', 'sub')), may hold values from -0.125 to 0.125
- cluster_transfer: float32 [32, 64, 64], P(('branch', 'sub')), may hold values from -0.375 to 0.375
- branch_index: int32 [8, 4], P('branch'), may hold values from 0 to 7, as said below
- branch_blocks: float32 [8, 4, 64, 64], P('branch'), may hold values from -0.375 to 0.375
Outputs:
- product: float32 [1152, 16, 128], P(('branch', 'sub'))
Inputs may be any that keep to these rules, and one draw needn't show every extreme that they name: `near_index`: entry 0 of row l is l itself; every entry of row l lies within 36 of l. `coupling_index`: every entry of row l lies within 36 of l. `branch_index`: the entries of a row are distinct and differ from the row's own branch cluster.
All inputs are finite; a program needn't handle non-finite values.
Results may differ from a plain program's by a relative error of at most 0.000067.
Values sent between devices are 32-bit elements; how exact they have to be, the bound alone decides.
No kernel may reach another device: no remote copies, remote signals or barrier semaphores. Data moves between devices by JAX's collectives and lax.ppermute only.
A program may use at most 64 MiB of HBM per device.

v0:
```python
import jax
import jax.numpy as jnp
from jax import lax
from jax.sharding import PartitionSpec as P

highest = lax.Precision.HIGHEST


def with_halo(block, sides, width):
    for axis, dim in sides:
        count = lax.axis_size(axis)
        forward = [(i, i + 1) for i in range(count - 1)]
        backward = [(target, source) for source, target in forward]
        low = lax.ppermute(
            lax.slice_in_dim(block, block.shape[dim] - width, None, axis=dim), axis, forward
        )
        high = lax.ppermute(lax.slice_in_dim(block, 0, width, axis=dim), axis, backward)
        block = jnp.concatenate([low, block, high], axis=dim)
    return block


def per_device(
    vectors,
    leaf_basis,
    near_index,
    near_blocks,
    coupling_index,
    coupling_blocks,
    leaf_transfer,
    cluster_transfer,
    branch_index,
    branch_blocks,
):
    leaf_count = vectors.shape[0]
    coeffs = jnp.einsum("lrp,lvp->lvr", leaf_basis, vectors, precision=highest)
    wide_points = with_halo(vectors, ((("branch", "sub"), 0),), leaf_count)
    wide_coeffs = with_halo(coeffs, ((("branch", "sub"), 0),), leaf_count)
    anchor = lax.axis_index(("branch", "sub")) * leaf_count - leaf_count
    near_rows = jnp.take(wide_points, near_index - anchor, axis=0)
    near_part = jnp.einsum("lkpq,lkvq->lvp", near_blocks, near_rows, precision=highest)
    coupled_rows = jnp.take(wide_coeffs, coupling_index - anchor, axis=0)
    leaf_far = jnp.einsum("lkrs,lkvs->lvr", coupling_blocks, coupled_rows, precision=highest)
    cluster = jnp.einsum("crs,cvs->vr", leaf_transfer, coeffs, precision=highest)
    share = jnp.einsum("rt,vt->vr", cluster_transfer[0], cluster, precision=highest)
    branch_node = lax.psum(share, "sub")
    nodes = lax.all_gather(branch_node[None], "branch", axis=0, tiled=True)
    chosen = jnp.take(nodes, branch_index[0], axis=0)
    branch_far = jnp.einsum("krs,kvs->vr", branch_blocks[0], chosen, precision=highest)
    cluster_down = jnp.einsum("rt,vr->vt", cluster_transfer[0], branch_far, precision=highest)
    leaf_total = leaf_far + jnp.einsum(
        "crs,vr->cvs", leaf_transfer, cluster_down, precision=highest
    )
    return near_part + jnp.einsum("lrp,lvr->lvp", leaf_basis, leaf_total, precision=highest)


def solution(mesh):
    in_specs = (
        P(("branch", "sub"), None, None),
        P(("branch", "sub"), None, None),
        P(("branch", "sub"), None),
        P(("branch", "sub"), None, None, None),
        P(("branch", "sub"), None),
        P(("branch", "sub"), None, None, None),
        P(("branch", "sub"), None, None),
        P(("branch", "sub"), None, None),
        P("branch", None),
        P("branch", None, None, None),
    )
    out_specs = P(("branch", "sub"), None, None)
    return jax.shard_map(
        per_device, mesh=mesh, in_specs=in_specs, out_specs=out_specs, check_vma=False
    )
```

profile of v0, /device:TPU:0, one launch (start us, length us, event | category | flops | bytes accessed | tf_op | source)
XLA Modules:
  0.0 85.8 jit_solution(6049992877514666596)
XLA Ops:
  0.0 0.0 copy-start
  0.0 0.0 copy-start.9
  0.0 0.0 copy-start.8
  0.0 0.0 copy-start.1
  0.0 1.2 %copy-done = f32[36,64,128]{2,1,0:T(8,128)S(1)} copy-done((f32[36,64,128]{2,1,0:T(8,128)S(1)}, f32[36,64,128]{2,1,0:T(8,128)}, u32[]{:S(2)}) %copy-start) | copy-done | bytes 1179672
  1.3 2.9 %fusion.21 = f32[36,16,64]{2,1,0:T(8,128)S(1)} fusion(f32[36,16,128]{2,1,0:T(8,128)} %param.10, f32[36,64,128]{2,1,0:T(8,128)S(1)} %copy-done), kind=kOutput, calls=%fused_computation.41 | convolution fusion | flops 56623104 | bytes 1622016 | tf_op jit(solution)/shard_map/lrp,lvp->lvr/dot_general | solution.py:35
  4.2 0.0 copy-start.3
  4.2 1.4 %collective-permute-start.3 = (f32[36,16,64]{2,1,0:T(8,128)S(1)}, f32[36,16,64]{2,1,0:T(8,128)S(1)}, u32[]{:S(2)}, u32[]{:S(2)}) collective-permute-start(f32[36,16,64]{2,1,0:T(8,128)S(1)} %fusion.21), channel_id=1, source_target_pairs={{1,0},{2,1},{3,2},{4,3},{5,4},{6,5},{7,6},{8,7},{9,8},{10,9},{11,1... | collective-permute-start | bytes 442376 | tf_op jit(solution)/shard_map/ppermute | solution.py:17
  5.6 3.8 %collective-permute-start.2 = (f32[36,16,64]{2,1,0:T(8,128)S(1)}, f32[36,16,64]{2,1,0:T(8,128)}, u32[]{:S(2)}, u32[]{:S(2)}) collective-permute-start(f32[36,16,64]{2,1,0:T(8,128)S(1)} %fusion.21), channel_id=1, source_target_pairs={{0,1},{1,2},{2,3},{3,4},{4,5},{5,6},{6,7},{7,8},{8,9},{9,10},{10,1... | collective-permute-start | bytes 442376 | tf_op jit(solution)/shard_map/ppermute | solution.py:14
  9.4 1.3 %collective-permute-start.1 = (f32[36,16,128]{2,1,0:T(8,128)}, f32[36,16,128]{2,1,0:T(8,128)}, u32[]{:S(2)}, u32[]{:S(2)}) collective-permute-start(f32[36,16,128]{2,1,0:T(8,128)} %param.10), channel_id=1, source_target_pairs={{1,0},{2,1},{3,2},{4,3},{5,4},{6,5},{7,6},{8,7},{9,8},{10,9},{11,1... | collective-permute-start | bytes 884744 | tf_op jit(solution)/shard_map/ppermute | solution.py:17
  10.6 5.1 %collective-permute-start = (f32[36,16,128]{2,1,0:T(8,128)}, f32[36,16,128]{2,1,0:T(8,128)}, u32[]{:S(2)}, u32[]{:S(2)}) collective-permute-start(f32[36,16,128]{2,1,0:T(8,128)} %param.10), channel_id=1, source_target_pairs={{0,1},{1,2},{2,3},{3,4},{4,5},{5,6},{6,7},{7,8},{8,9},{9,10},{10,1... | collective-permute-start | bytes 884744 | tf_op jit(solution)/shard_map/ppermute | solution.py:14
  15.8 0.0 copy-done.9
  15.8 0.0 copy-done.7
  15.8 0.0 copy-done.8
  15.9 0.1 copy.21
  16.0 0.1 reshape.54
  16.1 0.1 copy.19
  16.2 0.1 reshape.46
  16.3 0.0 copy-done.1
  16.3 1.0 %convolution_bitcast_fusion.2 = f32[16,64]{1,0:T(8,128)S(1)} fusion(f32[36,16,64]{2,1,0:T(8,128)S(1)} %fusion.21, f32[36,64,64]{2,1,0:T(8,128)S(1)} %copy-done.1), kind=kOutput, calls=%fused_computation.10 | convolution fusion | flops 28311552 | bytes 741376 | tf_op jit(solution)/shard_map/crs,cvs->vr/dot_general | solution.py:43
  17.3 0.0 copy-done.3
  17.3 0.2 convolution_bitcast_fusion.5
  17.5 9.8 %psum.7 = f32[1,16,64]{2,1,0:T(8,128)S(1)} all-reduce(f32[1,16,64]{2,1,0:T(8,128)S(1)} %convolution_bitcast_fusion.5), channel_id=1, replica_groups=mesh['branch'=8,'sub'=4] {'sub'}, use_global_device_ids=true, to_apply=%region_0.1 | all-reduce | flops 1024 | bytes 8192 | tf_op jit(solution)/shard_map/psum | solution.py:45
  27.3 31.7 %all_gather.3 = f32[8,16,64]{2,1,0:T(8,128)S(1)} all-gather(f32[1,16,64]{2,1,0:T(8,128)S(1)} %psum.7), channel_id=1, replica_groups=mesh['branch'=8,'sub'=4] {'branch'}, dimensions={0}, use_global_device_ids=true | all-gather | bytes 36864 | tf_op jit(solution)/shard_map/all_gather | solution.py:46
  58.9 0.5 gather_fusion.2
  59.5 0.0 copy-done.4
  59.5 0.2 convolution_bitcast_fusion.4
  59.8 0.7 copy.20
  60.5 0.7 copy.18
  61.2 0.1 convolution_bitcast_fusion.3
  61.3 0.0 collective-permute-done.3
  61.3 0.0 copy-start.2
  61.3 0.7 copy-done.2
  62.0 0.0 collective-permute-done.2
  62.1 1.1 %pad_maximum_fusion.1 = f32[108,16,64]{2,1,0:T(8,128)S(1)} fusion(f32[36,16,64]{2,1,0:T(8,128)} %copy-done.2, f32[36,16,64]{2,1,0:T(8,128)S(1)} %fusion.21, f32[36,16,64]{2,1,0:T(8,128)} %collective-permute-done.2), kind=kLoop, calls=%fused_computation.15 | loop fusion | flops 221184 | bytes 884736 | tf_op jit(solution)/shard_map/concatenate | solution.py:18
  63.2 0.0 copy-start.6
  63.2 1.8 %gather_fusion.1 = f32[144,16,64]{2,1,0:T(8,128)} fusion(f32[108,16,64]{2,1,0:T(8,128)S(1)} %pad_maximum_fusion.1, s32[1024]{0:T(1024)S(1)} %pad_clamp_fusion.1), kind=kCustom, calls=%fused_computation.1 | custom fusion | bytes 1180224 | tf_op jit(solution)/shard_map/jit(_take)/gather | solution.py:41
  65.0 0.0 copy-done.6
  65.0 6.7 %fusion.3 = f32[36,16,64]{2,1,0:T(8,128)S(1)} fusion(f32[36,4,64,64]{3,2,1,0:T(8,128)} %param.15, f32[36,4,16,64]{3,2,1,0:T(8,128)} %bitcast.46, pred[36,4]{1,0:T(8,128)(4,1)S(1)} %copy-done.6), kind=kOutput, calls=%fused_computation.8 | convolution fusion | flops 113393664 | bytes 3096720 | tf_op jit(solution)/shard_map/lkrs,lkvs->lvr/dot_general | solution.py:42
  71.7 0.7 fusion.2
  72.4 0.0 collective-permute-done.1
  72.4 0.0 collective-permute-done
  72.4 1.2 %pad_maximum_fusion = f32[108,16,128]{2,1,0:T(8,128)S(1)} fusion(f32[36,16,128]{2,1,0:T(8,128)} %collective-permute-done.1, f32[36,16,128]{2,1,0:T(8,128)} %param.10, f32[36,16,128]{2,1,0:T(8,128)} %collective-permute-done), kind=kLoop, calls=%fused_computation.14 | loop fusion | flops 442368 | bytes 1769472 | tf_op jit(solution)/shard_map/concatenate | solution.py:18
  73.6 0.0 copy-start.5
  73.6 0.7 gather_fusion
  74.3 0.0 copy-done.5
  74.4 9.6 %convolution_bitcast_fusion.1 = f32[36,16,128]{2,1,0:T(8,128)S(1)} fusion(f32[36,3,128,128]{3,2,1,0:T(8,128)} %param.13, f32[36,3,16,128]{3,2,1,0:T(8,128)S(1)} %bitcast.47, pred[36,3]{1,0:T(8,128)(4,1)S(1)} %copy-done.5), kind=kOutput, calls=%fused_computation.9 | convolution fusion | flops 339959808 | bytes 8257644 | tf_op jit(solution)/shard_map/lkpq,lkvq->lvp/dot_general | solution.py:40
  84.0 1.9 %convolution_add_fusion = f32[36,16,128]{2,1,0:T(8,128)} fusion(f32[36,16,128]{2,1,0:T(8,128)S(1)} %convolution_bitcast_fusion.1, f32[36,16,64]{2,1,0:T(8,128)S(1)} %fusion.2, f32[36,64,128]{2,1,0:T(8,128)S(1)} %copy-done), kind=kOutput, calls=%fused_computation.5 | convolution fusion | flops 56696832 | bytes 1916928 | tf_op jit(solution)/shard_map/lrp,lvr->lvp/dot_general | solution.py:53
  (9 shorter events, 0.1 us)
Async XLA Ops:
  0.0 1.3 %copy-start = (f32[36,64,128]{2,1,0:T(8,128)S(1)}, f32[36,64,128]{2,1,0:T(8,128)}, u32[]{:S(2)}) copy-start(f32[36,64,128]{2,1,0:T(8,128)} %param.11) | copy-start | bytes 3538948
  0.0 15.8 %copy-start.9 = (s32[1,4]{1,0:T(1,128)S(1)}, s32[1,4]{1,0:T(1,128)}, u32[]{:S(2)}) copy-start(s32[1,4]{1,0:T(1,128)} %param.18) | copy-start | bytes 52
  0.0 15.8 %copy-start.7 = (s32[36,3]{0,1:T(4,128)S(1)}, s32[36,3]{0,1:T(4,128)}, u32[]{:S(2)}) copy-start(s32[36,3]{0,1:T(4,128)} %param.12) | copy-start | bytes 1300
  0.0 15.8 %copy-start.8 = (s32[36,4]{0,1:T(4,128)S(1)}, s32[36,4]{0,1:T(4,128)}, u32[]{:S(2)}) copy-start(s32[36,4]{0,1:T(4,128)} %param.14) | copy-start | bytes 1732
  0.0 16.3 %copy-start.1 = (f32[36,64,64]{2,1,0:T(8,128)S(1)}, f32[36,64,64]{2,1,0:T(8,128)}, u32[]{:S(2)}) copy-start(f32[36,64,64]{2,1,0:T(8,128)} %param.16) | copy-start | bytes 1769476
  4.2 13.2 %copy-start.3 = (f32[1,64,64]{2,1,0:T(8,128)S(1)}, f32[1,64,64]{2,1,0:T(8,128)}, u32[]{:S(2)}) copy-start(f32[1,64,64]{2,1,0:T(8,128)} %param.17) | copy-start | bytes 49156
  4.2 55.3 %copy-start.4 = (f32[1,4,64,64]{3,2,1,0:T(8,128)S(1)}, f32[1,4,64,64]{3,2,1,0:T(8,128)}, u32[]{:S(2)}) copy-start(f32[1,4,64,64]{3,2,1,0:T(8,128)} %param.19) | copy-start | bytes 196612
  4.2 57.2 %collective-permute-start.3 = (f32[36,16,64]{2,1,0:T(8,128)S(1)}, f32[36,16,64]{2,1,0:T(8,128)S(1)}, u32[]{:S(2)}, u32[]{:S(2)}) collective-permute-start(f32[36,16,64]{2,1,0:T(8,128)S(1)} %fusion.21), channel_id=1, source_target_pairs={{1,0},{2,1},{3,2},{4,3},{5,4},{6,5},{7,6},{8,7},{9,8},{10,9},{11,1... | collective-permute-start | bytes 442376 | tf_op jit(solution)/shard_map/ppermute | solution.py:17
  5.6 56.5 %collective-permute-start.2 = (f32[36,16,64]{2,1,0:T(8,128)S(1)}, f32[36,16,64]{2,1,0:T(8,128)}, u32[]{:S(2)}, u32[]{:S(2)}) collective-permute-start(f32[36,16,64]{2,1,0:T(8,128)S(1)} %fusion.21), channel_id=1, source_target_pairs={{0,1},{1,2},{2,3},{3,4},{4,5},{5,6},{6,7},{7,8},{8,9},{9,10},{10,1... | collective-permute-start | bytes 442376 | tf_op jit(solution)/shard_map/ppermute | solution.py:14
  9.4 63.0 %collective-permute-start.1 = (f32[36,16,128]{2,1,0:T(8,128)}, f32[36,16,128]{2,1,0:T(8,128)}, u32[]{:S(2)}, u32[]{:S(2)}) collective-permute-start(f32[36,16,128]{2,1,0:T(8,128)} %param.10), channel_id=1, source_target_pairs={{1,0},{2,1},{3,2},{4,3},{5,4},{6,5},{7,6},{8,7},{9,8},{10,9},{11,1... | collective-permute-start | bytes 884744 | tf_op jit(solution)/shard_map/ppermute | solution.py:17
  10.6 61.8 %collective-permute-start = (f32[36,16,128]{2,1,0:T(8,128)}, f32[36,16,128]{2,1,0:T(8,128)}, u32[]{:S(2)}, u32[]{:S(2)}) collective-permute-start(f32[36,16,128]{2,1,0:T(8,128)} %param.10), channel_id=1, source_target_pairs={{0,1},{1,2},{2,3},{3,4},{4,5},{5,6},{6,7},{7,8},{8,9},{9,10},{10,1... | collective-permute-start | bytes 884744 | tf_op jit(solution)/shard_map/ppermute | solution.py:14
  61.3 0.7 copy-start.2
  63.2 1.8 %copy-start.6 = (pred[36,4]{1,0:T(8,128)(4,1)S(1)}, pred[36,4]{1,0:T(8,128)(4,1)}, u32[]{:S(2)}) copy-start(pred[36,4]{1,0:T(8,128)(4,1)} %copy.20) | copy-start | bytes 436
  73.6 0.7 copy-start.5
where the time goes:
time: 86.2 us; the launch traced here: 85.8 us
  blocking collectives  41.4 us (48%)
  matrix products  23.3 us (27%)
  starting transfers between devices  11.6 us (13%)
  local copies, waits for them, and re-layouts  6.88 us (8%)
  other arithmetic  2.4 us (3%)
    all_gather x1, blocking collectives, per_device(): nodes = lax.all_gather(branch_node[None], 'branch', axis=0, tiled=True)  31.7 us
    psum x1, blocking collectives, per_device(): branch_node = lax.psum(share, 'sub')  9.78 us
    dot_general x1, matrix products, per_device(): jnp.einsum('lkpq,lkvq->lvp', near_blocks, near_rows, precision=highest)  9.62 us
    ppermute x2, starting transfers between devices, with_halo(): lax.ppermute(lax.slice_in_dim(block, block.shape[dim] - width, None, axis...  8.89 us
    dot_general x1, matrix products, per_device(): jnp.einsum('lkrs,lkvs->lvr', coupling_blocks, coupled_rows, precision=hig...  6.69 us
    dot_general x1, matrix products, per_device(): coeffs = jnp.einsum('lrp,lvp->lvr', leaf_basis, vectors, precision=highest)  2.89 us
    ppermute x2, starting transfers between devices, with_halo(): lax.ppermute(lax.slice_in_dim(block, 0, width, axis=dim), axis, backward)  2.7 us
    concatenate x2, other arithmetic, with_halo(): block = jnp.concatenate([low, block, high], axis=dim)  2.31 us
  transfers between devices with their start and end apart: 4, of which 0 were waited for; matrix products, arithmetic and copies ran while one was open for 17% of the time, Pallas kernels for 0%

commit v1 on v0

v1 whole, which is shorter than its diff:
```python
import jax
import jax.numpy as jnp
from jax import lax
from jax.experimental import pallas as pl
from jax.experimental.pallas import tpu as pltpu
from jax.sharding import PartitionSpec as P

AXES = ("branch", "sub")
f32, bf16 = jnp.float32, jnp.bfloat16
VMEM = pl.BlockSpec(memory_space=pltpu.VMEM)
SMEM = pl.BlockSpec(memory_space=pltpu.SMEM)
ANY = pl.BlockSpec(memory_space=pl.ANY)
PARAMS = pltpu.CompilerParams(vmem_limit_bytes=16 * 1024 * 1024)
CHUNKS = 2


def halves(x):
    high = x.astype(bf16)
    return high, (x - high.astype(f32)).astype(bf16)


def rows_of(x):
    high, low = halves(x)
    return jnp.concatenate(
        [jnp.concatenate([high, high], axis=1), jnp.concatenate([low, jnp.zeros_like(low)], axis=1)], axis=0
    )


def weights_of(w, axis):
    return jnp.concatenate(halves(w), axis=axis)


def both(x):
    n = x.shape[0] // 2
    return x[:n] + x[n:]


def dot_nt(a, b):
    return lax.dot_general(a, b, (((1,), (1,)), ((), ())), preferred_element_type=f32)


def dot_nn(a, b):
    return lax.dot_general(a, b, (((1,), (0,)), ((), ())), preferred_element_type=f32)


def pack(x):
    n = x.shape[0] // 2
    return jnp.concatenate([x[:n], x[n:]], axis=1)


def unpack(x):
    w = x.shape[1] // 2
    return jnp.concatenate([x[:, :w], x[:, w:]], axis=0)


def stream(sources, targets, sems):
    chunks = sems.shape[0]
    size = targets[0].shape[0] // chunks
    parts = []
    for c in range(chunks):
        part = pl.ds(c * size, size)
        copies = [
            pltpu.make_async_copy(src.at[part], dst.at[part], sems.at[c, i])
            for i, (src, dst) in enumerate(zip(sources, targets))
        ]
        for copy in copies:
            copy.start()
        parts.append((range(c * size, (c + 1) * size), copies))
    return parts


def wait_all(copies):
    for copy in copies:
        copy.wait()


def three(dot, a, weight):
    n = a.shape[0]
    rows = jnp.concatenate(halves(a), axis=0)
    high, low = halves(weight)
    wide = dot(rows, high)
    return wide[:n] + wide[n:] + dot(rows[:n], low)


def up_kernel(
    vectors_hbm, basis_hbm, transfer_hbm, top_hbm, blocks_hbm,
    share, folded, vectors, basis, blocks, transfer, top, sems, top_sem, block_sem,
):
    leaves, rank, points = basis.shape
    parts = stream((basis_hbm, transfer_hbm, vectors_hbm), (basis, transfer, vectors), sems)
    top_copy = pltpu.make_async_copy(top_hbm, top, top_sem)
    top_copy.start()
    block_copy = pltpu.make_async_copy(blocks_hbm.at[:, 0], blocks, block_sem)
    block_copy.start()
    for part, copies in parts:
        wait_all(copies)
        for l in part:
            high, low = halves(three(dot_nn, transfer[l], basis[l]))
            folded[l // 2, :, (l % 2) * points : (l % 2 + 1) * points] = jnp.concatenate([high, low, high], axis=0)
    cluster = None
    for first in range(0, leaves, 2):
        rows, weights = [], []
        for l in (first, first + 1):
            lane = pl.ds((l % 2) * points, points)
            weights += [folded[l // 2, :rank, lane], folded[l // 2, rank : 2 * rank, lane]]
            rows.append(rows_of(vectors[l]))
        term = dot_nt(jnp.concatenate(rows, axis=1), jnp.concatenate(weights, axis=1))
        cluster = term if cluster is None else cluster + term
    top_copy.wait()
    share[...] = pack(three(dot_nt, both(cluster), top[0]))
    block_copy.wait()


def coeffs_kernel(vectors, basis, coeffs):
    half = coeffs.shape[0]
    for j in range(half):
        pair = [both(dot_nt(rows_of(vectors[l]), weights_of(basis[l], 1))) for l in (j, j + half)]
        coeffs[j] = jnp.concatenate(pair, axis=1)


def sides(own, across, beside):
    n = own[1]
    odd = lax.rem(lax.axis_index("sub"), 2)
    return (own[0], n), (beside, 2 * n * (1 - odd)), (across, 2 * n * odd)


def first_leaf(leaves):
    return (lax.axis_index("branch") * lax.axis_size("sub") + lax.axis_index("sub")) * leaves - leaves


def turned_sum(rows, blocks):
    weights = jnp.concatenate([weights_of(block, 1) for block in blocks], axis=1)
    return both(dot_nt(weights, jnp.concatenate(rows, axis=1)).T)


def own_kernel(vectors, blocks, next_hbm, out, next_blocks, sem):
    copy = pltpu.make_async_copy(next_hbm, next_blocks, sem)
    copy.start()
    for l in range(blocks.shape[0]):
        out[l] = turned_sum([rows_of(vectors[l])], [blocks[l]])
    copy.wait()


def coupling_kernel(index, coeffs, across, beside, basis, near, blocks, next_hbm, out, next_blocks, split, far, sem):
    leaves, coup, rank = blocks.shape[:3]
    copy = pltpu.make_async_copy(next_hbm.at[:, pl.ds(1, next_blocks.shape[1])], next_blocks, sem)
    copy.start()
    half = leaves // 2
    left = lax.broadcasted_iota(jnp.int32, coeffs.shape[1:], 1) < rank
    for ref, base in sides((coeffs, leaves), across, beside):
        for j in range(half):
            two = ref[j]
            turned = pltpu.roll(two, rank, 1)
            for l, twice in ((j, jnp.where(left, two, turned)), (j + half, jnp.where(left, turned, two))):
                high = twice.astype(bf16)
                low = jnp.where(left, twice - high.astype(f32), 0.0).astype(bf16)
                split[base + l] = jnp.concatenate([high, low], axis=0)
    anchor = first_leaf(leaves)
    for l in range(leaves):
        rows = jnp.concatenate([split[index[k, l] - anchor] for k in range(coup)], axis=1)
        weights = jnp.concatenate([weights_of(blocks[l, k], 1) for k in range(coup)], axis=1)
        far[l] = both(dot_nt(rows, weights))
    for l in range(leaves):
        out[l] = near[l] + three(dot_nn, far[l], basis[l])
    copy.wait()


def last_kernel(
    near_index, branch_index, vectors, across, beside, nodes, branch_blocks, top, folded, partial, blocks, out, split
):
    leaves, others, points = blocks.shape[:3]
    branch = lax.axis_index("branch")
    far = None
    for k in range(branch_blocks.shape[1]):
        node = unpack(nodes[jnp.bitwise_xor(branch_index[0, k], branch)])
        term = three(dot_nt, node, branch_blocks[0, k])
        far = term if far is None else far + term
    high, low = halves(three(dot_nn, far, top[0]))
    down = jnp.concatenate([high, high, low], axis=1)
    for ref, base in sides((vectors, leaves), across, beside):
        for l in range(leaves):
            split[base + l] = rows_of(ref[l])
    anchor = first_leaf(leaves)
    for l in range(leaves):
        if l % 2 == 0:
            two = dot_nn(down, folded[l // 2])
        rows = [split[near_index[k + 1, l] - anchor] for k in range(others)]
        near = turned_sum(rows, [blocks[l, k] for k in range(others)])
        out[l] = partial[l] + near + two[:, (l % 2) * points : (l % 2 + 1) * points]


def in_hbm(*arrays):
    return [pltpu.with_memory_space_constraint(x, pltpu.HBM) for x in arrays]


def flip(x, mask, count):
    return lax.ppermute(x, AXES, [(i, i ^ mask) for i in range(count)])


def across_chips(beside, count):
    pairs = [(i, i + 2) for i in range(0, count - 2, 2)] + [(i + 3, i + 1) for i in range(0, count - 2, 2)]
    return lax.ppermute(beside, AXES, pairs + [(count - 2, count - 1), (1, 0)])


def per_device(
    vectors,
    leaf_basis,
    near_index,
    near_blocks,
    coupling_index,
    coupling_blocks,
    leaf_transfer,
    cluster_transfer,
    branch_index,
    branch_blocks,
):
    leaves, nv, points = vectors.shape
    rank = leaf_basis.shape[1]
    near = near_blocks.shape[1]
    half = leaves // 2
    members, branches = lax.axis_size("sub"), lax.axis_size("branch")
    count = members * branches
    sds = jax.ShapeDtypeStruct
    product = sds((leaves, nv, points), f32)

    vec_beside = flip(vectors, 1, count)

    share, folded, vectors_in, basis_in, own_blocks = pl.pallas_call(
        up_kernel,
        out_shape=(
            sds((nv // 2, 2 * rank), f32),
            sds((half, 3 * rank, 2 * points), bf16),
            product,
            sds(leaf_basis.shape, f32),
            sds((leaves, points, points), f32),
        ),
        in_specs=[ANY] * 5,
        out_specs=(VMEM,) * 5,
        scratch_shapes=[
            pltpu.VMEM(leaf_transfer.shape, f32),
            pltpu.VMEM(cluster_transfer.shape, f32),
            pltpu.SemaphoreType.DMA((CHUNKS, 3)),
            pltpu.SemaphoreType.DMA,
            pltpu.SemaphoreType.DMA,
        ],
        compiler_params=PARAMS,
        name="up",
    )(*in_hbm(vectors, leaf_basis, leaf_transfer, cluster_transfer, near_blocks))

    node = share + flip(share, 1, count)

    coeffs = pl.pallas_call(
        coeffs_kernel,
        out_shape=sds((half, nv, 2 * rank), f32),
        in_specs=[VMEM] * 2,
        out_specs=VMEM,
        compiler_params=PARAMS,
        name="coeffs",
    )(vectors_in, basis_in)
    coeff_beside = flip(coeffs, 1, count)
    coeff_across = across_chips(coeff_beside, count)
    vec_across = across_chips(vec_beside, count)

    bit = 2
    while bit < members:
        node = node + flip(node, bit + 1, count)
        bit *= 2
    nodes = node[None]
    while bit < count:
        nodes = jnp.concatenate([nodes, flip(nodes, bit + 1, count)], axis=0)
        bit *= 2

    own, coup_blocks = pl.pallas_call(
        own_kernel,
        out_shape=(product, sds(coupling_blocks.shape, f32)),
        in_specs=[VMEM, VMEM, ANY],
        out_specs=(VMEM, VMEM),
        scratch_shapes=[pltpu.SemaphoreType.DMA],
        compiler_params=PARAMS,
        name="near_own",
    )(vectors_in, own_blocks, *in_hbm(coupling_blocks))

    partial, other_blocks = pl.pallas_call(
        coupling_kernel,
        out_shape=(product, sds((leaves, near - 1, points, points), f32)),
        in_specs=[SMEM] + [VMEM] * 6 + [ANY],
        out_specs=(VMEM, VMEM),
        scratch_shapes=[
            pltpu.VMEM((3 * leaves, 2 * nv, 2 * rank), bf16),
            pltpu.VMEM((leaves, nv, rank), f32),
            pltpu.SemaphoreType.DMA,
        ],
        compiler_params=PARAMS,
        name="coupling",
    )(coupling_index.T, coeffs, coeff_across, coeff_beside, basis_in, own, coup_blocks, *in_hbm(near_blocks))

    return pl.pallas_call(
        last_kernel,
        out_shape=product,
        in_specs=[SMEM] * 2 + [VMEM] * 9,
        out_specs=VMEM,
        scratch_shapes=[pltpu.VMEM((3 * leaves, 2 * nv, 2 * points), bf16)],
        compiler_params=PARAMS,
        name="last",
    )(
        near_index.T, branch_index, vectors_in, vec_across, vec_beside, nodes, branch_blocks, cluster_transfer,
        folded, partial, other_blocks,
    )


def solution(mesh):
    lead = P(AXES)
    in_specs = (lead,) * 8 + (P("branch"),) * 2
    return jax.shard_map(per_device, mesh=mesh, in_specs=in_specs, out_specs=lead, check_vma=False)
```

time: 86.2 us -> 30 us (0.35)
  blocking collectives: 41.4 us -> 0 us
  matrix products: 23.3 us -> 0 us
  Pallas kernels: 0 us -> 13.2 us
  local copies, waits for them, and re-layouts: 6.88 us -> 0.02 us
  waiting for transfers between devices: 0.01 us -> 6.48 us
  other arithmetic: 2.4 us -> 0.01 us
  starting transfers between devices: 11.6 us -> 10.1 us
    all_gather x1 -> x0, blocking collectives: 31.7 us -> none  [per_device(): nodes = lax.all_gather(branch_node[None], 'branch', axis=0, tiled=True)]
    dot_general x9 -> x0, matrix products: 23.3 us -> none  [the longest x1 9.62 us: per_device(): jnp.einsum('lkpq,lkvq->lvp', near_blocks, near_rows, precision=highest)]
    pallas_call x0 -> x5, Pallas kernels: none -> 13.2 us  [the longest x1 4.17 us: per_device(): pl.pallas_call(coupling_kernel, out_shape=(product, sds((leaves, near - 1...]
    psum x1 -> x0, blocking collectives: 9.78 us -> none  [per_device(): branch_node = lax.psum(share, 'sub')]
    ppermute x4 -> x9, waiting for transfers between devices: 0.01 us -> 6.48 us  [the longest x7 5.49 us: flip(): return lax.ppermute(x, AXES, [(i, i ^ mask) for i in range(count)])]
    gather x3 -> x0, local copies, waits for them, and re-layouts: 3.09 us -> none  [the longest x1 1.82 us: per_device(): coupled_rows = jnp.take(wide_coeffs, coupling_index - anchor, axis=0)]
    concatenate x2 -> x3, other arithmetic: 2.31 us -> 0.01 us  [per_device(): nodes = jnp.concatenate([nodes, flip(nodes, bit + 1, count)], axis=0)]
    unnamed x20 -> x10, local copies, waits for them, and re-layouts: 1.99 us -> 0.02 us
  transfers between devices with their start and end apart: 4 -> 9, of which waited for: 0 -> 5; matrix products, arithmetic and copies ran while one was open for 17% -> 0% of each run, Pallas kernels for 0% -> 33%
where the time goes in v1:
time: 30 us; the launch traced here: 29.9 us
  Pallas kernels  13.2 us (44%)
  starting transfers between devices  10.1 us (34%)
  waiting for transfers between devices  6.48 us (22%)
    ppermute x7, starting transfers between devices, flip(): return lax.ppermute(x, AXES, [(i, i ^ mask) for i in range(count)])  7.01 us
    ppermute x7, waiting for transfers between devices, flip(): return lax.ppermute(x, AXES, [(i, i ^ mask) for i in range(count)])  5.49 us
    pallas_call x1, Pallas kernels, per_device(): pl.pallas_call(coupling_kernel, out_shape=(product, sds((leaves, near - 1...  4.17 us
    pallas_call x1, Pallas kernels, per_device(): pl.pallas_call(last_kernel, out_shape=product, in_specs=[SMEM] * 2 + [VME...  3.22 us
    ppermute x2, starting transfers between devices, across_chips(): return lax.ppermute(beside, AXES, pairs + [(count - 2, count - 1), (1, 0)])  3.05 us
    pallas_call x1, Pallas kernels, per_device(): pl.pallas_call(up_kernel, out_shape=(sds((nv // 2, 2 * rank), f32), sds((...  2.97 us
    pallas_call x1, Pallas kernels, per_device(): pl.pallas_call(own_kernel, out_shape=(product, sds(coupling_blocks.shape,...  2.36 us
    ppermute x2, waiting for transfers between devices, across_chips(): return lax.ppermute(beside, AXES, pairs + [(count - 2, count - 1), (1, 0)])  0.99 us
  transfers between devices with their start and end apart: 9, of which 5 were waited for; matrix products, arithmetic and copies ran while one was open for 0% of the time, Pallas kernels for 33%

profile of v1, /device:TPU:0, one launch (start us, length us, event | category | flops | bytes accessed | tf_op | source)
XLA Modules:
  0.0 29.9 jit_solution(12652700688595370923)
XLA Ops:
  0.0 0.5 %collective-permute-start = (f32[36,16,128]{2,1,0:T(8,128)}, f32[36,16,128]{2,1,0:T(8,128)S(1)}, u32[]{:S(2)}, u32[]{:S(2)}) collective-permute-start(f32[36,16,128]{2,1,0:T(8,128)} %vectors_hbm.1), channel_id=1, source_target_pairs={{0,1},{1,0},{2,3},{3,2},{4,5},{5,4},{6,7},{7,6},{8,9},{9,8},{10,11... | collective-permute-start | bytes 884744 | tf_op jit(solution)/shard_map/ppermute | solution.py:197
  0.5 3.0 %up.1 = (f32[8,128]{1,0:T(8,128)S(1)}, bf16[18,192,256]{2,1,0:T(8,128)(2,1)S(1)}, f32[36,16,128]{2,1,0:T(8,128)S(1)}, f32[36,64,128]{2,1,0:T(8,128)S(1)}, f32[36,128,128]{2,1,0:T(8,128)S(1)}) custom-call(f32[36,16,128]{2,1,0:T(8,128)} %vectors_hbm.1, f32[36,64,128]{2,1,0:T(8,128)} %basis_hbm.1, f32[36,64,64]{2,1,0:T(8,128)} %transfer_hbm.1, ...), custom_call_target="tpu_custom_call" | custom-call | tf_op jit(solution)/shard_map/up/pallas_call | solution.py:228
  3.4 0.1 collective-permute-start.2
  3.6 1.1 %collective-permute-done.2 = f32[8,128]{1,0:T(8,128)S(1)} collective-permute-done((f32[8,128]{1,0:T(8,128)S(1)}, f32[8,128]{1,0:T(8,128)S(1)}, u32[]{:S(2)}, u32[]{:S(2)}) %collective-permute-start.2) | collective-permute-done | bytes 4128 | tf_op jit(solution)/shard_map/ppermute | solution.py:197
  4.7 2.6 %collective-permute-start.3 = (f32[8,128]{1,0:T(8,128)S(1)}, f32[8,128]{1,0:T(8,128)S(1)}, u32[]{:S(2)}, u32[]{:S(2)}) collective-permute-start(f32[8,128]{1,0:T(8,128)S(1)} %add.6), channel_id=1, source_target_pairs={{0,3},{1,2},{2,1},{3,0},{4,7},{5,6},{6,5},{7,4},{8,11},{9,10},{10,... | collective-permute-start | bytes 12296 | tf_op jit(solution)/shard_map/ppermute | solution.py:197
  7.3 0.5 %coeffs.1 = f32[18,16,128]{2,1,0:T(8,128)S(1)} custom-call(f32[36,16,128]{2,1,0:T(8,128)S(1)} %get-tuple-element.14.vectors, f32[36,64,128]{2,1,0:T(8,128)S(1)} %get-tuple-element.17.basis), custom_call_target="tpu_custom_call" | custom-call | tf_op jit(solution)/shard_map/coeffs/pallas_call | solution.py:252
  7.8 0.2 collective-permute-start.7
  8.0 0.6 %collective-permute-done.3 = f32[8,128]{1,0:T(8,128)S(1)} collective-permute-done((f32[8,128]{1,0:T(8,128)S(1)}, f32[8,128]{1,0:T(8,128)S(1)}, u32[]{:S(2)}, u32[]{:S(2)}) %collective-permute-start.3) | collective-permute-done | bytes 4128 | tf_op jit(solution)/shard_map/ppermute | solution.py:197
  8.6 1.7 %collective-permute-start.4 = (f32[1,8,128]{2,1,0:T(8,128)S(1)}, f32[1,8,128]{2,1,0:T(8,128)S(1)}, u32[]{:S(2)}, u32[]{:S(2)}) collective-permute-start(f32[1,8,128]{2,1,0:T(8,128)S(1)} %add_bitcast_fusion), channel_id=1, source_target_pairs={{0,5},{1,4},{2,7},{3,6},{4,1},{5,0},{6,3},{7,2},{8,13},{9,12},{10,... | collective-permute-start | bytes 12296 | tf_op jit(solution)/shard_map/ppermute | solution.py:197
  10.3 0.0 collective-permute-done.beside
  10.3 1.5 %collective-permute-start.1 = (f32[36,16,128]{2,1,0:T(8,128)S(1)}, f32[36,16,128]{2,1,0:T(8,128)S(1)}, u32[]{:S(2)}, u32[]{:S(2)}) collective-permute-start(f32[36,16,128]{2,1,0:T(8,128)S(1)} %collective-permute-done.beside), channel_id=1, source_target_pairs={{0,2},{2,4},{4,6},{6,8},{8,10},{10,12},{12,14},{14,16},{16,18},{18... | collective-permute-start | bytes 884744 | tf_op jit(solution)/shard_map/ppermute | solution.py:202
  11.8 0.0 collective-permute-done.4
  11.8 1.6 %collective-permute-start.5 = (f32[2,8,128]{2,1,0:T(8,128)S(1)}, f32[2,8,128]{2,1,0:T(8,128)S(1)}, u32[]{:S(2)}, u32[]{:S(2)}) collective-permute-start(f32[2,8,128]{2,1,0:T(8,128)S(1)} %pad_maximum_fusion.2), channel_id=1, source_target_pairs={{0,9},{1,8},{2,11},{3,10},{4,13},{5,12},{6,15},{7,14},{8,1},{9,0},... | collective-permute-start | bytes 24584 | tf_op jit(solution)/shard_map/ppermute | solution.py:197
  13.4 0.0 collective-permute-done.7.beside
  13.4 1.5 %collective-permute-start.8 = (f32[18,16,128]{2,1,0:T(8,128)S(1)}, f32[18,16,128]{2,1,0:T(8,128)S(1)}, u32[]{:S(2)}, u32[]{:S(2)}) collective-permute-start(f32[18,16,128]{2,1,0:T(8,128)S(1)} %collective-permute-done.7.beside), channel_id=1, source_target_pairs={{0,2},{2,4},{4,6},{6,8},{8,10},{10,12},{12,14},{14,16},{16,18},{18... | collective-permute-start | bytes 442376 | tf_op jit(solution)/shard_map/ppermute | solution.py:202
  15.0 2.4 %collective-permute-done.5 = f32[2,8,128]{2,1,0:T(8,128)S(1)} collective-permute-done((f32[2,8,128]{2,1,0:T(8,128)S(1)}, f32[2,8,128]{2,1,0:T(8,128)S(1)}, u32[]{:S(2)}, u32[]{:S(2)}) %collective-permute-start.5) | collective-permute-done | bytes 8224 | tf_op jit(solution)/shard_map/ppermute | solution.py:197
  17.3 0.3 %collective-permute-start.6 = (f32[4,8,128]{2,1,0:T(8,128)S(1)}, f32[4,8,128]{2,1,0:T(8,128)S(1)}, u32[]{:S(2)}, u32[]{:S(2)}) collective-permute-start(f32[4,8,128]{2,1,0:T(8,128)S(1)} %pad_maximum_fusion.1), channel_id=1, source_target_pairs={{0,17},{1,16},{2,19},{3,18},{4,21},{5,20},{6,23},{7,22},{8,25},{9,... | collective-permute-start | bytes 49160 | tf_op jit(solution)/shard_map/ppermute | solution.py:197
  17.7 0.0 copy-start.2
  17.7 2.4 %near_own.1 = (f32[36,16,128]{2,1,0:T(8,128)S(1)}, f32[36,4,64,64]{3,2,1,0:T(8,128)S(1)}) custom-call(f32[36,16,128]{2,1,0:T(8,128)S(1)} %get-tuple-element.14.vectors, f32[36,128,128]{2,1,0:T(8,128)S(1)} %get-tuple-element.18.blocks, f32[36,4,64,64]{3,2,1,0:T(8,128)} %next_hbm.2), custom_call_target="tpu_custom_call" | custom-call | tf_op jit(solution)/shard_map/near_own/pallas_call | solution.py:273
  20.0 1.4 %collective-permute-done.6 = f32[4,8,128]{2,1,0:T(8,128)S(1)} collective-permute-done((f32[4,8,128]{2,1,0:T(8,128)S(1)}, f32[4,8,128]{2,1,0:T(8,128)S(1)}, u32[]{:S(2)}, u32[]{:S(2)}) %collective-permute-start.6) | collective-permute-done | bytes 16416 | tf_op jit(solution)/shard_map/ppermute | solution.py:197
  21.4 1.0 %collective-permute-done.8.across = f32[18,16,128]{2,1,0:T(8,128)S(1)} collective-permute-done((f32[18,16,128]{2,1,0:T(8,128)S(1)}, f32[18,16,128]{2,1,0:T(8,128)S(1)}, u32[]{:S(2)}, u32[]{:S(2)}) %collective-permute-start.8) | collective-permute-done | bytes 147488 | tf_op jit(solution)/shard_map/ppermute | solution.py:202
  22.4 0.0 copy-done.2
  22.4 0.0 copy-start
  22.4 0.0 copy-start.1
  22.4 0.0 copy-start.3
  22.4 0.0 copy-start.4
  22.4 4.2 %coupling.1 = (f32[36,16,128]{2,1,0:T(8,128)S(1)}, f32[36,2,128,128]{3,2,1,0:T(8,128)S(1)}) custom-call(s32[4,36]{1,0:T(4,128)S(1)} %bitcast.4, f32[18,16,128]{2,1,0:T(8,128)S(1)} %coeffs.1, f32[18,16,128]{2,1,0:T(8,128)S(1)} %collective-permute-done.8.across, f32[18,16,128]{2,1,0:T(8,128)S(1)} %collective-permute-done.7.beside, ...), custom_call_target="tpu_custom_call" | custom-call | tf_op jit(solution)/shard_map/coupling/pallas_call | solution.py:283
  26.6 0.0 collective-permute-done.1.across
  26.6 0.0 copy-done
  26.6 0.0 copy-done.1
  26.6 0.0 copy-done.3
  26.6 0.0 copy-done.4
  26.6 3.2 %last.1 = f32[36,16,128]{2,1,0:T(8,128)} custom-call(s32[3,36]{1,0:T(4,128)S(1)} %bitcast.5, s32[1,4]{1,0:T(1,128)S(1)} %copy-done.4, f32[36,16,128]{2,1,0:T(8,128)S(1)} %get-tuple-element.14.vectors, f32[36,16,128]{2,1,0:T(8,128)S(1)} %collective-permute-done.1.across, f32[36,16,128]{2,1,0:T(8,128)S(1)} %collective-permute-done.beside, ...), custom_call_target="tpu_custom_call" | custom-call | tf_op jit(solution)/shard_map/last/pallas_call | solution.py:297
  (5 shorter events, 0.0 us)
Async XLA Ops:
  0.0 10.3 %collective-permute-start = (f32[36,16,128]{2,1,0:T(8,128)}, f32[36,16,128]{2,1,0:T(8,128)S(1)}, u32[]{:S(2)}, u32[]{:S(2)}) collective-permute-start(f32[36,16,128]{2,1,0:T(8,128)} %vectors_hbm.1), channel_id=1, source_target_pairs={{0,1},{1,0},{2,3},{3,2},{4,5},{5,4},{6,7},{7,6},{8,9},{9,8},{10,11... | collective-permute-start | bytes 884744 | tf_op jit(solution)/shard_map/ppermute | solution.py:197
  3.4 1.2 %collective-permute-start.2 = (f32[8,128]{1,0:T(8,128)S(1)}, f32[8,128]{1,0:T(8,128)S(1)}, u32[]{:S(2)}, u32[]{:S(2)}) collective-permute-start(f32[8,128]{1,0:T(8,128)S(1)} %get-tuple-element.15), channel_id=1, source_target_pairs={{0,1},{1,0},{2,3},{3,2},{4,5},{5,4},{6,7},{7,6},{8,9},{9,8},{10,11... | collective-permute-start | bytes 12296 | tf_op jit(solution)/shard_map/ppermute | solution.py:197
  4.7 4.0 %collective-permute-start.3 = (f32[8,128]{1,0:T(8,128)S(1)}, f32[8,128]{1,0:T(8,128)S(1)}, u32[]{:S(2)}, u32[]{:S(2)}) collective-permute-start(f32[8,128]{1,0:T(8,128)S(1)} %add.6), channel_id=1, source_target_pairs={{0,3},{1,2},{2,1},{3,0},{4,7},{5,6},{6,5},{7,4},{8,11},{9,10},{10,... | collective-permute-start | bytes 12296 | tf_op jit(solution)/shard_map/ppermute | solution.py:197
  7.8 5.7 %collective-permute-start.7 = (f32[18,16,128]{2,1,0:T(8,128)S(1)}, f32[18,16,128]{2,1,0:T(8,128)S(1)}, u32[]{:S(2)}, u32[]{:S(2)}) collective-permute-start(f32[18,16,128]{2,1,0:T(8,128)S(1)} %coeffs.1), channel_id=1, source_target_pairs={{0,1},{1,0},{2,3},{3,2},{4,5},{5,4},{6,7},{7,6},{8,9},{9,8},{10,11... | collective-permute-start | bytes 442376 | tf_op jit(solution)/shard_map/ppermute | solution.py:197
  8.6 3.2 %collective-permute-start.4 = (f32[1,8,128]{2,1,0:T(8,128)S(1)}, f32[1,8,128]{2,1,0:T(8,128)S(1)}, u32[]{:S(2)}, u32[]{:S(2)}) collective-permute-start(f32[1,8,128]{2,1,0:T(8,128)S(1)} %add_bitcast_fusion), channel_id=1, source_target_pairs={{0,5},{1,4},{2,7},{3,6},{4,1},{5,0},{6,3},{7,2},{8,13},{9,12},{10,... | collective-permute-start | bytes 12296 | tf_op jit(solution)/shard_map/ppermute | solution.py:197
  10.3 16.3 %collective-permute-start.1 = (f32[36,16,128]{2,1,0:T(8,128)S(1)}, f32[36,16,128]{2,1,0:T(8,128)S(1)}, u32[]{:S(2)}, u32[]{:S(2)}) collective-permute-start(f32[36,16,128]{2,1,0:T(8,128)S(1)} %collective-permute-done.beside), channel_id=1, source_target_pairs={{0,2},{2,4},{4,6},{6,8},{8,10},{10,12},{12,14},{14,16},{16,18},{18... | collective-permute-start | bytes 884744 | tf_op jit(solution)/shard_map/ppermute | solution.py:202
  11.8 5.5 %collective-permute-start.5 = (f32[2,8,128]{2,1,0:T(8,128)S(1)}, f32[2,8,128]{2,1,0:T(8,128)S(1)}, u32[]{:S(2)}, u32[]{:S(2)}) collective-permute-start(f32[2,8,128]{2,1,0:T(8,128)S(1)} %pad_maximum_fusion.2), channel_id=1, source_target_pairs={{0,9},{1,8},{2,11},{3,10},{4,13},{5,12},{6,15},{7,14},{8,1},{9,0},... | collective-permute-start | bytes 24584 | tf_op jit(solution)/shard_map/ppermute | solution.py:197
  13.4 9.0 %collective-permute-start.8 = (f32[18,16,128]{2,1,0:T(8,128)S(1)}, f32[18,16,128]{2,1,0:T(8,128)S(1)}, u32[]{:S(2)}, u32[]{:S(2)}) collective-permute-start(f32[18,16,128]{2,1,0:T(8,128)S(1)} %collective-permute-done.7.beside), channel_id=1, source_target_pairs={{0,2},{2,4},{4,6},{6,8},{8,10},{10,12},{12,14},{14,16},{16,18},{18... | collective-permute-start | bytes 442376 | tf_op jit(solution)/shard_map/ppermute | solution.py:202
  17.3 4.1 %collective-permute-start.6 = (f32[4,8,128]{2,1,0:T(8,128)S(1)}, f32[4,8,128]{2,1,0:T(8,128)S(1)}, u32[]{:S(2)}, u32[]{:S(2)}) collective-permute-start(f32[4,8,128]{2,1,0:T(8,128)S(1)} %pad_maximum_fusion.1), channel_id=1, source_target_pairs={{0,17},{1,16},{2,19},{3,18},{4,21},{5,20},{6,23},{7,22},{8,25},{9,... | collective-permute-start | bytes 49160 | tf_op jit(solution)/shard_map/ppermute | solution.py:197
  17.7 4.7 %copy-start.2 = (s32[36,4]{0,1:T(4,128)S(1)}, s32[36,4]{0,1:T(4,128)}, u32[]{:S(2)}) copy-start(s32[36,4]{0,1:T(4,128)} %param.14) | copy-start | bytes 1732
  22.4 4.2 %copy-start = (f32[1,4,64,64]{3,2,1,0:T(8,128)S(1)}, f32[1,4,64,64]{3,2,1,0:T(8,128)}, u32[]{:S(2)}) copy-start(f32[1,4,64,64]{3,2,1,0:T(8,128)} %branch_blocks.1) | copy-start | bytes 196612
  22.4 4.2 %copy-start.1 = (f32[1,64,64]{2,1,0:T(8,128)S(1)}, f32[1,64,64]{2,1,0:T(8,128)}, u32[]{:S(2)}) copy-start(f32[1,64,64]{2,1,0:T(8,128)} %top.1) | copy-start | bytes 49156
  22.4 4.2 %copy-start.3 = (s32[36,3]{0,1:T(4,128)S(1)}, s32[36,3]{0,1:T(4,128)}, u32[]{:S(2)}) copy-start(s32[36,3]{0,1:T(4,128)} %param.12) | copy-start | bytes 1300
  22.4 4.2 %copy-start.4 = (s32[1,4]{1,0:T(1,128)S(1)}, s32[1,4]{1,0:T(1,128)}, u32[]{:S(2)}) copy-start(s32[1,4]{1,0:T(1,128)} %branch_index.1) | copy-start | bytes 52

commit v2 on v1

--- a/solution.py
+++ b/solution.py
@@ -69,6 +69,10 @@
     return parts
 
 
+def then(body):
+    pl.when(lax.axis_index("sub") >= 0)(body)
+
+
 def wait_all(copies):
     for copy in copies:
         copy.wait()
@@ -92,22 +96,26 @@
     top_copy.start()
     block_copy = pltpu.make_async_copy(blocks_hbm.at[:, 0], blocks, block_sem)
     block_copy.start()
-    for part, copies in parts:
-        wait_all(copies)
-        for l in part:
-            high, low = halves(three(dot_nn, transfer[l], basis[l]))
-            folded[l // 2, :, (l % 2) * points : (l % 2 + 1) * points] = jnp.concatenate([high, low, high], axis=0)
-    cluster = None
-    for first in range(0, leaves, 2):
-        rows, weights = [], []
-        for l in (first, first + 1):
-            lane = pl.ds((l % 2) * points, points)
-            weights += [folded[l // 2, :rank, lane], folded[l // 2, rank : 2 * rank, lane]]
-            rows.append(rows_of(vectors[l]))
-        term = dot_nt(jnp.concatenate(rows, axis=1), jnp.concatenate(weights, axis=1))
-        cluster = term if cluster is None else cluster + term
-    top_copy.wait()
-    share[...] = pack(three(dot_nt, both(cluster), top[0]))
+
+    @then
+    def _():
+        cluster = None
+        for part, copies in parts:
+            wait_all(copies)
+            for l in part:
+                high, low = halves(three(dot_nn, transfer[l], basis[l]))
+                folded[l // 2, :, (l % 2) * points : (l % 2 + 1) * points] = jnp.concatenate([high, low, high], axis=0)
+            for first in part[::2]:
+                rows, weights = [], []
+                for l in (first, first + 1):
+                    lane = pl.ds((l % 2) * points, points)
+                    weights += [folded[l // 2, :rank, lane], folded[l // 2, rank : 2 * rank, lane]]
+                    rows.append(rows_of(vectors[l]))
+                term = dot_nt(jnp.concatenate(rows, axis=1), jnp.concatenate(weights, axis=1))
+                cluster = term if cluster is None else cluster + term
+        top_copy.wait()
+        share[...] = pack(three(dot_nt, both(cluster), top[0]))
+
     block_copy.wait()
 
 
@@ -134,45 +142,61 @@
 
 
 def own_kernel(vectors, blocks, next_hbm, out, next_blocks, sem):
-    copy = pltpu.make_async_copy(next_hbm, next_blocks, sem)
+    count, others = next_blocks.shape[:2]
+    copy = pltpu.make_async_copy(next_hbm.at[pl.ds(0, count), pl.ds(1, others)], next_blocks, sem)
     copy.start()
-    for l in range(blocks.shape[0]):
-        out[l] = turned_sum([rows_of(vectors[l])], [blocks[l]])
+
+    @then
+    def _():
+        for l in range(blocks.shape[0]):
+            out[l] = turned_sum([rows_of(vectors[l])], [blocks[l]])
+
     copy.wait()
 
 
-def coupling_kernel(index, coeffs, across, beside, basis, near, blocks, next_hbm, out, next_blocks, split, far, sem):
-    leaves, coup, rank = blocks.shape[:3]
-    copy = pltpu.make_async_copy(next_hbm.at[:, pl.ds(1, next_blocks.shape[1])], next_blocks, sem)
+def coupling_kernel(
+    index, coeffs, across, beside, basis, near, blocks, next_hbm, out, next_blocks, split, far, sem
+):
+    leaves, (coup, rank) = basis.shape[0], blocks.shape[1:3]
+    count, others = next_blocks.shape[:2]
+    copy = pltpu.make_async_copy(next_hbm.at[pl.ds(leaves - count, count), pl.ds(1, others)], next_blocks, sem)
     copy.start()
-    half = leaves // 2
-    left = lax.broadcasted_iota(jnp.int32, coeffs.shape[1:], 1) < rank
-    for ref, base in sides((coeffs, leaves), across, beside):
-        for j in range(half):
-            two = ref[j]
-            turned = pltpu.roll(two, rank, 1)
-            for l, twice in ((j, jnp.where(left, two, turned)), (j + half, jnp.where(left, turned, two))):
-                high = twice.astype(bf16)
-                low = jnp.where(left, twice - high.astype(f32), 0.0).astype(bf16)
-                split[base + l] = jnp.concatenate([high, low], axis=0)
-    anchor = first_leaf(leaves)
-    for l in range(leaves):
-        rows = jnp.concatenate([split[index[k, l] - anchor] for k in range(coup)], axis=1)
-        weights = jnp.concatenate([weights_of(blocks[l, k], 1) for k in range(coup)], axis=1)
-        far[l] = both(dot_nt(rows, weights))
-    for l in range(leaves):
-        out[l] = near[l] + three(dot_nn, far[l], basis[l])
+
+    @then
+    def _():
+        half = leaves // 2
+        left = lax.broadcasted_iota(jnp.int32, coeffs.shape[1:], 1) < rank
+        for ref, base in sides((coeffs, leaves), across, beside):
+            for j in range(half):
+                two = ref[j]
+                turned = pltpu.roll(two, rank, 1)
+                for l, twice in ((j, jnp.where(left, two, turned)), (j + half, jnp.where(left, turned, two))):
+                    high = twice.astype(bf16)
+                    low = jnp.where(left, twice - high.astype(f32), 0.0).astype(bf16)
+                    split[base + l] = jnp.concatenate([high, low], axis=0)
+        anchor = first_leaf(leaves)
+        for l in range(leaves):
+            rows = jnp.concatenate([split[index[k, l] - anchor] for k in range(coup)], axis=1)
+            weights = jnp.concatenate([weights_of(blocks[l, k], 1) for k in range(coup)], axis=1)
+            far[l] = both(dot_nt(rows, weights))
+        for l in range(leaves):
+            out[l] = near[l] + three(dot_nn, far[l], basis[l])
+
     copy.wait()
 
 
 def last_kernel(
-    near_index, branch_index, vectors, across, beside, nodes, branch_blocks, top, folded, partial, blocks, out, split
+    near_index, branch_index, vectors, across, beside, nodes, far_nodes, branch_blocks, top, folded, partial, first_blocks,
+    blocks, out, split,
 ):
-    leaves, others, points = blocks.shape[:3]
+    leaves, early, (others, points) = out.shape[0], first_blocks.shape[0], blocks.shape[1:3]
     branch = lax.axis_index("branch")
+    known = nodes.shape[0]
     far = None
     for k in range(branch_blocks.shape[1]):
-        node = unpack(nodes[jnp.bitwise_xor(branch_index[0, k], branch)])
+        slot = jnp.bitwise_xor(branch_index[0, k], branch)
+        place = lax.rem(slot, known)
+        node = unpack(jnp.where(slot < known, nodes[place], far_nodes[place]))
         term = three(dot_nt, node, branch_blocks[0, k])
         far = term if far is None else far + term
     high, low = halves(three(dot_nn, far, top[0]))
@@ -185,7 +209,8 @@
         if l % 2 == 0:
             two = dot_nn(down, folded[l // 2])
         rows = [split[near_index[k + 1, l] - anchor] for k in range(others)]
-        near = turned_sum(rows, [blocks[l, k] for k in range(others)])
+        block = first_blocks.at[l] if l < early else blocks.at[l - early]
+        near = turned_sum(rows, [block[k] for k in range(others)])
         out[l] = partial[l] + near + two[:, (l % 2) * points : (l % 2 + 1) * points]
 
 
@@ -247,8 +272,8 @@
         name="up",
     )(*in_hbm(vectors, leaf_basis, leaf_transfer, cluster_transfer, near_blocks))
 
-    node = share + flip(share, 1, count)
-
+    share, coupling_blocks = lax.optimization_barrier((share, coupling_blocks))
+    first = flip(share, 1, count)
     coeffs = pl.pallas_call(
         coeffs_kernel,
         out_shape=sds((half, nv, 2 * rank), f32),
@@ -258,31 +283,35 @@
         name="coeffs",
     )(vectors_in, basis_in)
     coeff_beside = flip(coeffs, 1, count)
-    coeff_across = across_chips(coeff_beside, count)
-    vec_across = across_chips(vec_beside, count)
+    node = share + first
+    node, coeffs = lax.optimization_barrier((node, coeffs))
+    early = 2 * (leaves // 3)
+    own, first_blocks = pl.pallas_call(
+        own_kernel,
+        out_shape=(product, sds((early, near - 1, points, points), f32)),
+        in_specs=[VMEM] * 2 + [ANY],
+        out_specs=(VMEM, VMEM),
+        scratch_shapes=[pltpu.SemaphoreType.DMA],
+        compiler_params=PARAMS,
+        name="near_own",
+    )(vectors_in, own_blocks, *in_hbm(near_blocks))
 
     bit = 2
     while bit < members:
         node = node + flip(node, bit + 1, count)
         bit *= 2
+    coeff_across = across_chips(coeff_beside, count)
     nodes = node[None]
-    while bit < count:
+    vec_across = across_chips(vec_beside, count)
+    while 2 * bit < count:
         nodes = jnp.concatenate([nodes, flip(nodes, bit + 1, count)], axis=0)
         bit *= 2
-
-    own, coup_blocks = pl.pallas_call(
-        own_kernel,
-        out_shape=(product, sds(coupling_blocks.shape, f32)),
-        in_specs=[VMEM, VMEM, ANY],
-        out_specs=(VMEM, VMEM),
-        scratch_shapes=[pltpu.SemaphoreType.DMA],
-        compiler_params=PARAMS,
-        name="near_own",
-    )(vectors_in, own_blocks, *in_hbm(coupling_blocks))
+    nodes, own = lax.optimization_barrier((nodes, own))
+    far_nodes = flip(nodes, bit + 1, count)
 
     partial, other_blocks = pl.pallas_call(
         coupling_kernel,
-        out_shape=(product, sds((leaves, near - 1, points, points), f32)),
+        out_shape=(product, sds((leaves - early, near - 1, points, points), f32)),
         in_specs=[SMEM] + [VMEM] * 6 + [ANY],
         out_specs=(VMEM, VMEM),
         scratch_shapes=[
@@ -292,19 +321,22 @@
         ],
         compiler_params=PARAMS,
         name="coupling",
-    )(coupling_index.T, coeffs, coeff_across, coeff_beside, basis_in, own, coup_blocks, *in_hbm(near_blocks))
+    )(
+        coupling_index.T, coeffs, coeff_across, coeff_beside, basis_in, own, coupling_blocks,
+        *in_hbm(near_blocks),
+    )
 
     return pl.pallas_call(
         last_kernel,
         out_shape=product,
-        in_specs=[SMEM] * 2 + [VMEM] * 9,
+        in_specs=[SMEM] * 2 + [VMEM] * 11,
         out_specs=VMEM,
         scratch_shapes=[pltpu.VMEM((3 * leaves, 2 * nv, 2 * points), bf16)],
         compiler_params=PARAMS,
         name="last",
     )(
-        near_index.T, branch_index, vectors_in, vec_across, vec_beside, nodes, branch_blocks, cluster_transfer,
-        folded, partial, other_blocks,
+        near_index.T, branch_index, vectors_in, vec_across, vec_beside, nodes, far_nodes, branch_blocks,
+        cluster_transfer, folded, partial, first_blocks, other_blocks,
     )
 
 

time: 30 us -> 25.1 us (0.84)
  Pallas kernels: 13.2 us -> 10.6 us
  waiting for transfers between devices: 6.48 us -> 4.12 us
    pallas_call x2, Pallas kernels: 6.52 us -> 4.03 us  [the longest x1 2.05 us: per_device(): pl.pallas_call(own_kernel, out_shape=(product, sds((early, near - 1, poin...]
    ppermute x7, waiting for transfers between devices: 5.49 us -> 4.11 us  [flip(): return lax.ppermute(x, AXES, [(i, i ^ mask) for i in range(count)])]
    ppermute x2, starting transfers between devices: 3.05 us -> 1.75 us  [across_chips(): return lax.ppermute(beside, AXES, pairs + [(count - 2, count - 1), (1, 0)])]
    ppermute x7, starting transfers between devices: 7.01 us -> 8.29 us  [flip(): return lax.ppermute(x, AXES, [(i, i ^ mask) for i in range(count)])]
    ppermute x2, waiting for transfers between devices: 0.99 us -> 0.01 us  [across_chips(): return lax.ppermute(beside, AXES, pairs + [(count - 2, count - 1), (1, 0)])]
  transfers between devices with their start and end apart: 9 -> 9, of which waited for: 5 -> 4; matrix products, arithmetic and copies ran while one was open for 0% -> 0% of each run, Pallas kernels for 33% -> 30%
where the time goes in v2:
time: 25.1 us; the launch traced here: 25 us
  Pallas kernels  10.6 us (42%)
  starting transfers between devices  10 us (40%)
  waiting for transfers between devices  4.12 us (16%)
    ppermute x7, starting transfers between devices, flip(): return lax.ppermute(x, AXES, [(i, i ^ mask) for i in range(count)])  8.29 us
    ppermute x7, waiting for transfers between devices, flip(): return lax.ppermute(x, AXES, [(i, i ^ mask) for i in range(count)])  4.11 us
    pallas_call x1, Pallas kernels, per_device(): pl.pallas_call(last_kernel, out_shape=product, in_specs=[SMEM] * 2 + [VME...  3.23 us
    pallas_call x1, Pallas kernels, per_device(): pl.pallas_call(up_kernel, out_shape=(sds((nv // 2, 2 * rank), f32), sds((...  2.9 us
    pallas_call x1, Pallas kernels, per_device(): pl.pallas_call(own_kernel, out_shape=(product, sds((early, near - 1, poin...  2.05 us
    pallas_call x1, Pallas kernels, per_device(): pl.pallas_call(coupling_kernel, out_shape=(product, sds((leaves - early,...  1.99 us
    ppermute x2, starting transfers between devices, across_chips(): return lax.ppermute(beside, AXES, pairs + [(count - 2, count - 1), (1, 0)])  1.75 us
  transfers between devices with their start and end apart: 9, of which 4 were waited for; matrix products, arithmetic and copies ran while one was open for 0% of the time, Pallas kernels for 30%

profile of v2, /device:TPU:0, one launch (start us, length us, event | category | flops | bytes accessed | tf_op | source)
XLA Modules:
  0.0 25.0 jit_solution(7892648713044033752)
XLA Ops:
  0.0 0.5 %collective-permute-start = (f32[36,16,128]{2,1,0:T(8,128)}, f32[36,16,128]{2,1,0:T(8,128)S(1)}, u32[]{:S(2)}, u32[]{:S(2)}) collective-permute-start(f32[36,16,128]{2,1,0:T(8,128)} %vectors_hbm.1), channel_id=1, source_target_pairs={{0,1},{1,0},{2,3},{3,2},{4,5},{5,4},{6,7},{7,6},{8,9},{9,8},{10,11... | collective-permute-start | bytes 884744 | tf_op jit(solution)/shard_map/ppermute | solution.py:222
  0.5 2.9 %up.1 = (f32[8,128]{1,0:T(8,128)S(1)}, bf16[18,192,256]{2,1,0:T(8,128)(2,1)S(1)}, f32[36,16,128]{2,1,0:T(8,128)S(1)}, f32[36,64,128]{2,1,0:T(8,128)S(1)}, f32[36,128,128]{2,1,0:T(8,128)S(1)}) custom-call(f32[36,16,128]{2,1,0:T(8,128)} %vectors_hbm.1, f32[36,64,128]{2,1,0:T(8,128)} %basis_hbm.1, f32[36,64,64]{2,1,0:T(8,128)} %transfer_hbm.1, ...), custom_call_target="tpu_custom_call" | custom-call | tf_op jit(solution)/shard_map/up/pallas_call | solution.py:253
  3.4 0.1 collective-permute-start.2
  3.5 0.5 %coeffs.1 = f32[18,16,128]{2,1,0:T(8,128)S(1)} custom-call(f32[36,16,128]{2,1,0:T(8,128)S(1)} %get-tuple-element.20.vectors, f32[36,64,128]{2,1,0:T(8,128)S(1)} %get-tuple-element.23.basis), custom_call_target="tpu_custom_call" | custom-call | tf_op jit(solution)/shard_map/coeffs/pallas_call | solution.py:277
  4.0 0.6 %collective-permute-done.2 = f32[8,128]{1,0:T(8,128)S(1)} collective-permute-done((f32[8,128]{1,0:T(8,128)S(1)}, f32[8,128]{1,0:T(8,128)S(1)}, u32[]{:S(2)}, u32[]{:S(2)}) %collective-permute-start.2) | collective-permute-done | bytes 4128 | tf_op jit(solution)/shard_map/ppermute | solution.py:222
  4.6 2.6 %collective-permute-start.3 = (f32[8,128]{1,0:T(8,128)S(1)}, f32[8,128]{1,0:T(8,128)S(1)}, u32[]{:S(2)}, u32[]{:S(2)}) collective-permute-start(f32[8,128]{1,0:T(8,128)S(1)} %add.6), channel_id=1, source_target_pairs={{0,3},{1,2},{2,1},{3,0},{4,7},{5,6},{6,5},{7,4},{8,11},{9,10},{10,... | collective-permute-start | bytes 12296 | tf_op jit(solution)/shard_map/ppermute | solution.py:222
  7.2 0.2 collective-permute-start.7
  7.4 0.0 collective-permute-done.beside
  7.4 0.2 collective-permute-start.1
  7.6 0.9 %collective-permute-done.3 = f32[8,128]{1,0:T(8,128)S(1)} collective-permute-done((f32[8,128]{1,0:T(8,128)S(1)}, f32[8,128]{1,0:T(8,128)S(1)}, u32[]{:S(2)}, u32[]{:S(2)}) %collective-permute-start.3) | collective-permute-done | bytes 4128 | tf_op jit(solution)/shard_map/ppermute | solution.py:222
  8.6 1.7 %collective-permute-start.4 = (f32[1,8,128]{2,1,0:T(8,128)S(1)}, f32[1,8,128]{2,1,0:T(8,128)S(1)}, u32[]{:S(2)}, u32[]{:S(2)}) collective-permute-start(f32[1,8,128]{2,1,0:T(8,128)S(1)} %add_bitcast_fusion), channel_id=1, source_target_pairs={{0,5},{1,4},{2,7},{3,6},{4,1},{5,0},{6,3},{7,2},{8,13},{9,12},{10,... | collective-permute-start | bytes 12296 | tf_op jit(solution)/shard_map/ppermute | solution.py:222
  10.2 0.0 collective-permute-done.7.beside
  10.2 1.5 %collective-permute-start.8 = (f32[18,16,128]{2,1,0:T(8,128)S(1)}, f32[18,16,128]{2,1,0:T(8,128)S(1)}, u32[]{:S(2)}, u32[]{:S(2)}) collective-permute-start(f32[18,16,128]{2,1,0:T(8,128)S(1)} %collective-permute-done.7.beside), channel_id=1, source_target_pairs={{0,2},{2,4},{4,6},{6,8},{8,10},{10,12},{12,14},{14,16},{16,18},{18... | collective-permute-start | bytes 442376 | tf_op jit(solution)/shard_map/ppermute | solution.py:227
  11.8 1.6 %collective-permute-done.4 = f32[1,8,128]{2,1,0:T(8,128)S(1)} collective-permute-done((f32[1,8,128]{2,1,0:T(8,128)S(1)}, f32[1,8,128]{2,1,0:T(8,128)S(1)}, u32[]{:S(2)}, u32[]{:S(2)}) %collective-permute-start.4) | collective-permute-done | bytes 4128 | tf_op jit(solution)/shard_map/ppermute | solution.py:222
  13.4 0.1 collective-permute-start.5
  13.5 0.0 slice-start
  13.5 0.0 slice-start.1
  13.5 0.0 copy-start.2
  13.5 2.0 %near_own.1 = (f32[36,16,128]{2,1,0:T(8,128)S(1)}, f32[24,2,128,128]{3,2,1,0:T(8,128)S(1)}) custom-call(f32[36,16,128]{2,1,0:T(8,128)S(1)} %get-tuple-element.20.vectors, f32[36,128,128]{2,1,0:T(8,128)S(1)} %get-tuple-element.25.blocks, f32[36,3,128,128]{3,2,1,0:T(8,128)} %next_hbm.3), custom_call_target="tpu_custom_call" | custom-call | tf_op jit(solution)/shard_map/near_own/pallas_call | solution.py:289
  15.5 0.9 %collective-permute-done.5 = f32[2,8,128]{2,1,0:T(8,128)S(1)} collective-permute-done((f32[2,8,128]{2,1,0:T(8,128)S(1)}, f32[2,8,128]{2,1,0:T(8,128)S(1)}, u32[]{:S(2)}, u32[]{:S(2)}) %collective-permute-start.5) | collective-permute-done | bytes 8224 | tf_op jit(solution)/shard_map/ppermute | solution.py:222
  16.5 3.2 %collective-permute-start.6 = (f32[4,8,128]{2,1,0:T(8,128)S(1)}, f32[4,8,128]{2,1,0:T(8,128)S(1)}, u32[]{:S(2)}, u32[]{:S(2)}) collective-permute-start(f32[4,8,128]{2,1,0:T(8,128)S(1)} %pad_maximum_fusion.nodes), channel_id=1, source_target_pairs={{0,17},{1,16},{2,19},{3,18},{4,21},{5,20},{6,23},{7,22},{8,25},{9,... | collective-permute-start | bytes 49160 | tf_op jit(solution)/shard_map/ppermute | solution.py:222
  19.6 0.0 collective-permute-done.8.across
  19.6 0.0 slice-done
  19.6 0.0 slice-done.1
  19.6 0.0 copy-done.2
  19.6 0.0 copy-start
  19.7 0.0 copy-start.1
  19.7 0.0 copy-start.3
  19.7 0.0 copy-start.4
  19.7 2.0 %coupling.1 = (f32[36,16,128]{2,1,0:T(8,128)S(1)}, f32[12,2,128,128]{3,2,1,0:T(8,128)S(1)}) custom-call(s32[4,36]{1,0:T(4,128)S(1)} %bitcast.6, f32[18,16,128]{2,1,0:T(8,128)S(1)} %coeffs.1, f32[18,16,128]{2,1,0:T(8,128)S(1)} %collective-permute-done.8.across, f32[18,16,128]{2,1,0:T(8,128)S(1)} %collective-permute-done.7.beside, ...), custom_call_target="tpu_custom_call" | custom-call | tf_op jit(solution)/shard_map/coupling/pallas_call | solution.py:312
  21.7 0.0 collective-permute-done.6.far_nodes
  21.7 0.0 collective-permute-done.1.across
  21.7 0.0 copy-done
  21.7 0.0 copy-done.1
  21.7 0.0 copy-done.3
  21.7 0.0 copy-done.4
  21.7 3.2 %last.1 = f32[36,16,128]{2,1,0:T(8,128)} custom-call(s32[3,36]{1,0:T(4,128)S(1)} %bitcast.7, s32[1,4]{1,0:T(1,128)S(1)} %copy-done.4, f32[36,16,128]{2,1,0:T(8,128)S(1)} %get-tuple-element.20.vectors, f32[36,16,128]{2,1,0:T(8,128)S(1)} %collective-permute-done.1.across, f32[36,16,128]{2,1,0:T(8,128)S(1)} %collective-permute-done.beside, ...), custom_call_target="tpu_custom_call" | custom-call | tf_op jit(solution)/shard_map/last/pallas_call | solution.py:329
  (5 shorter events, 0.0 us)
Async XLA Ops:
  0.0 7.4 %collective-permute-start = (f32[36,16,128]{2,1,0:T(8,128)}, f32[36,16,128]{2,1,0:T(8,128)S(1)}, u32[]{:S(2)}, u32[]{:S(2)}) collective-permute-start(f32[36,16,128]{2,1,0:T(8,128)} %vectors_hbm.1), channel_id=1, source_target_pairs={{0,1},{1,0},{2,3},{3,2},{4,5},{5,4},{6,7},{7,6},{8,9},{9,8},{10,11... | collective-permute-start | bytes 884744 | tf_op jit(solution)/shard_map/ppermute | solution.py:222
  3.4 1.2 %collective-permute-start.2 = (f32[8,128]{1,0:T(8,128)S(1)}, f32[8,128]{1,0:T(8,128)S(1)}, u32[]{:S(2)}, u32[]{:S(2)}) collective-permute-start(f32[8,128]{1,0:T(8,128)S(1)} %get-tuple-element.22), channel_id=1, source_target_pairs={{0,1},{1,0},{2,3},{3,2},{4,5},{5,4},{6,7},{7,6},{8,9},{9,8},{10,11... | collective-permute-start | bytes 12296 | tf_op jit(solution)/shard_map/ppermute | solution.py:222
  4.6 4.0 %collective-permute-start.3 = (f32[8,128]{1,0:T(8,128)S(1)}, f32[8,128]{1,0:T(8,128)S(1)}, u32[]{:S(2)}, u32[]{:S(2)}) collective-permute-start(f32[8,128]{1,0:T(8,128)S(1)} %add.6), channel_id=1, source_target_pairs={{0,3},{1,2},{2,1},{3,0},{4,7},{5,6},{6,5},{7,4},{8,11},{9,10},{10,... | collective-permute-start | bytes 12296 | tf_op jit(solution)/shard_map/ppermute | solution.py:222
  7.2 3.0 %collective-permute-start.7 = (f32[18,16,128]{2,1,0:T(8,128)S(1)}, f32[18,16,128]{2,1,0:T(8,128)S(1)}, u32[]{:S(2)}, u32[]{:S(2)}) collective-permute-start(f32[18,16,128]{2,1,0:T(8,128)S(1)} %coeffs.1), channel_id=1, source_target_pairs={{0,1},{1,0},{2,3},{3,2},{4,5},{5,4},{6,7},{7,6},{8,9},{9,8},{10,11... | collective-permute-start | bytes 442376 | tf_op jit(solution)/shard_map/ppermute | solution.py:222
  7.4 14.3 %collective-permute-start.1 = (f32[36,16,128]{2,1,0:T(8,128)S(1)}, f32[36,16,128]{2,1,0:T(8,128)S(1)}, u32[]{:S(2)}, u32[]{:S(2)}) collective-permute-start(f32[36,16,128]{2,1,0:T(8,128)S(1)} %collective-permute-done.beside), channel_id=1, source_target_pairs={{0,2},{2,4},{4,6},{6,8},{8,10},{10,12},{12,14},{14,16},{16,18},{18... | collective-permute-start | bytes 884744 | tf_op jit(solution)/shard_map/ppermute | solution.py:227
  8.6 4.8 %collective-permute-start.4 = (f32[1,8,128]{2,1,0:T(8,128)S(1)}, f32[1,8,128]{2,1,0:T(8,128)S(1)}, u32[]{:S(2)}, u32[]{:S(2)}) collective-permute-start(f32[1,8,128]{2,1,0:T(8,128)S(1)} %add_bitcast_fusion), channel_id=1, source_target_pairs={{0,5},{1,4},{2,7},{3,6},{4,1},{5,0},{6,3},{7,2},{8,13},{9,12},{10,... | collective-permute-start | bytes 12296 | tf_op jit(solution)/shard_map/ppermute | solution.py:222
  10.2 9.4 %collective-permute-start.8 = (f32[18,16,128]{2,1,0:T(8,128)S(1)}, f32[18,16,128]{2,1,0:T(8,128)S(1)}, u32[]{:S(2)}, u32[]{:S(2)}) collective-permute-start(f32[18,16,128]{2,1,0:T(8,128)S(1)} %collective-permute-done.7.beside), channel_id=1, source_target_pairs={{0,2},{2,4},{4,6},{6,8},{8,10},{10,12},{12,14},{14,16},{16,18},{18... | collective-permute-start | bytes 442376 | tf_op jit(solution)/shard_map/ppermute | solution.py:227
  13.4 3.1 %collective-permute-start.5 = (f32[2,8,128]{2,1,0:T(8,128)S(1)}, f32[2,8,128]{2,1,0:T(8,128)S(1)}, u32[]{:S(2)}, u32[]{:S(2)}) collective-permute-start(f32[2,8,128]{2,1,0:T(8,128)S(1)} %pad_maximum_fusion.1), channel_id=1, source_target_pairs={{0,9},{1,8},{2,11},{3,10},{4,13},{5,12},{6,15},{7,14},{8,1},{9,0},... | collective-permute-start | bytes 24584 | tf_op jit(solution)/shard_map/ppermute | solution.py:222
  13.5 6.2 %slice-start = ((s8[4718592]{0:T(1024)(128)(4,1)}), s8[4194304]{0:T(1024)(128)(4,1)S(1)}, s32[]{:S(2)}) async-start(s8[4718592]{0:T(1024)(128)(4,1)} %bitcast.4), calls=%async_computation | async-start | bytes 8388608
  13.5 6.2 %slice-start.1 = ((s8[4718592]{0:T(1024)(128)(4,1)}), s8[524288]{0:T(1024)(128)(4,1)S(1)}, s32[]{:S(2)}) async-start(s8[4718592]{0:T(1024)(128)(4,1)} %bitcast.4), calls=%async_computation.1 | async-start | bytes 1048576
  13.5 6.2 %copy-start.2 = (s32[36,4]{0,1:T(4,128)S(1)}, s32[36,4]{0,1:T(4,128)}, u32[]{:S(2)}) copy-start(s32[36,4]{0,1:T(4,128)} %param.14) | copy-start | bytes 1732
  16.5 5.2 %collective-permute-start.6 = (f32[4,8,128]{2,1,0:T(8,128)S(1)}, f32[4,8,128]{2,1,0:T(8,128)S(1)}, u32[]{:S(2)}, u32[]{:S(2)}) collective-permute-start(f32[4,8,128]{2,1,0:T(8,128)S(1)} %pad_maximum_fusion.nodes), channel_id=1, source_target_pairs={{0,17},{1,16},{2,19},{3,18},{4,21},{5,20},{6,23},{7,22},{8,25},{9,... | collective-permute-start | bytes 49160 | tf_op jit(solution)/shard_map/ppermute | solution.py:222
  19.6 2.1 %copy-start = (f32[1,4,64,64]{3,2,1,0:T(8,128)S(1)}, f32[1,4,64,64]{3,2,1,0:T(8,128)}, u32[]{:S(2)}) copy-start(f32[1,4,64,64]{3,2,1,0:T(8,128)} %branch_blocks.1) | copy-start | bytes 196612
  19.7 2.1 %copy-start.1 = (f32[1,64,64]{2,1,0:T(8,128)S(1)}, f32[1,64,64]{2,1,0:T(8,128)}, u32[]{:S(2)}) copy-start(f32[1,64,64]{2,1,0:T(8,128)} %top.1) | copy-start | bytes 49156
  19.7 2.1 %copy-start.3 = (s32[36,3]{0,1:T(4,128)S(1)}, s32[36,3]{0,1:T(4,128)}, u32[]{:S(2)}) copy-start(s32[36,3]{0,1:T(4,128)} %param.12) | copy-start | bytes 1300
  19.7 2.1 %copy-start.4 = (s32[1,4]{1,0:T(1,128)S(1)}, s32[1,4]{1,0:T(1,128)}, u32[]{:S(2)}) copy-start(s32[1,4]{1,0:T(1,128)} %branch_index.1) | copy-start | bytes 52

commit v3 on v2

--- a/solution.py
+++ b/solution.py
@@ -141,27 +141,28 @@
     return both(dot_nt(weights, jnp.concatenate(rows, axis=1)).T)
 
 
-def own_kernel(vectors, blocks, next_hbm, out, next_blocks, sem):
-    count, others = next_blocks.shape[:2]
-    copy = pltpu.make_async_copy(next_hbm.at[pl.ds(0, count), pl.ds(1, others)], next_blocks, sem)
-    copy.start()
-
-    @then
-    def _():
-        for l in range(blocks.shape[0]):
-            out[l] = turned_sum([rows_of(vectors[l])], [blocks[l]])
-
-    copy.wait()
+def dot_tn(a, b):
+    return lax.dot_general(a, b, (((0,), (0,)), ((), ())), preferred_element_type=f32)
+
+
+def own_kernel(vectors, blocks, branch_blocks, top, out, down):
+    high, low = halves(top[0])
+    for k in range(branch_blocks.shape[1]):
+        first, second = halves(branch_blocks[0, k])
+        down[k] = dot_tn(first, high) + dot_tn(second, high) + dot_tn(first, low)
+    for l in range(blocks.shape[0]):
+        out[l] = turned_sum([rows_of(vectors[l])], [blocks[l]])
+
+
+def weights_kernel(blocks, out):
+    for l in range(blocks.shape[0]):
+        out[l] = jnp.concatenate([weights_of(blocks[l, k], 1) for k in range(blocks.shape[1])], axis=1)
 
 
 def coupling_kernel(
-    index, coeffs, across, beside, basis, near, blocks, next_hbm, out, next_blocks, split, far, sem
+    index, coeffs, across, beside, basis, near, blocks, out, split, far
 ):
-    leaves, (coup, rank) = basis.shape[0], blocks.shape[1:3]
-    count, others = next_blocks.shape[:2]
-    copy = pltpu.make_async_copy(next_hbm.at[pl.ds(leaves - count, count), pl.ds(1, others)], next_blocks, sem)
-    copy.start()
-
+    leaves, (coup, rank) = basis.shape[0], (index.shape[0], basis.shape[1])
     @then
     def _():
         half = leaves // 2
@@ -177,41 +178,43 @@
         anchor = first_leaf(leaves)
         for l in range(leaves):
             rows = jnp.concatenate([split[index[k, l] - anchor] for k in range(coup)], axis=1)
-            weights = jnp.concatenate([weights_of(blocks[l, k], 1) for k in range(coup)], axis=1)
+            weights = blocks[l]
             far[l] = both(dot_nt(rows, weights))
         for l in range(leaves):
             out[l] = near[l] + three(dot_nn, far[l], basis[l])
 
-    copy.wait()
-
-
 def last_kernel(
-    near_index, branch_index, vectors, across, beside, nodes, far_nodes, branch_blocks, top, folded, partial, first_blocks,
-    blocks, out, split,
+    near_index, branch_index, vectors, across, beside, nodes, far_nodes, steps, folded, partial, blocks,
+    out_hbm, split, out, sems,
 ):
-    leaves, early, (others, points) = out.shape[0], first_blocks.shape[0], blocks.shape[1:3]
+    leaves, near, points = blocks.shape[:3]
     branch = lax.axis_index("branch")
     known = nodes.shape[0]
     far = None
-    for k in range(branch_blocks.shape[1]):
+    for k in range(steps.shape[0]):
         slot = jnp.bitwise_xor(branch_index[0, k], branch)
         place = lax.rem(slot, known)
         node = unpack(jnp.where(slot < known, nodes[place], far_nodes[place]))
-        term = three(dot_nt, node, branch_blocks[0, k])
+        term = three(dot_nn, node, steps[k])
         far = term if far is None else far + term
-    high, low = halves(three(dot_nn, far, top[0]))
+    high, low = halves(far)
     down = jnp.concatenate([high, high, low], axis=1)
     for ref, base in sides((vectors, leaves), across, beside):
         for l in range(leaves):
             split[base + l] = rows_of(ref[l])
     anchor = first_leaf(leaves)
+    size, copies = leaves // sems.shape[0], []
     for l in range(leaves):
         if l % 2 == 0:
             two = dot_nn(down, folded[l // 2])
-        rows = [split[near_index[k + 1, l] - anchor] for k in range(others)]
-        block = first_blocks.at[l] if l < early else blocks.at[l - early]
-        near = turned_sum(rows, [block[k] for k in range(others)])
-        out[l] = partial[l] + near + two[:, (l % 2) * points : (l % 2 + 1) * points]
+        rows = [split[near_index[k, l] - anchor] for k in range(1, near)]
+        others = turned_sum(rows, [blocks[l, k] for k in range(1, near)])
+        out[l] = partial[l] + others + two[:, (l % 2) * points : (l % 2 + 1) * points]
+        if (l + 1) % size == 0:
+            part = pl.ds(l + 1 - size, size)
+            copies.append(pltpu.make_async_copy(out.at[part], out_hbm.at[part], sems.at[l // size]))
+            copies[-1].start()
+    wait_all(copies)
 
 
 def in_hbm(*arrays):
@@ -272,7 +275,6 @@
         name="up",
     )(*in_hbm(vectors, leaf_basis, leaf_transfer, cluster_transfer, near_blocks))
 
-    share, coupling_blocks = lax.optimization_barrier((share, coupling_blocks))
     first = flip(share, 1, count)
     coeffs = pl.pallas_call(
         coeffs_kernel,
@@ -285,16 +287,14 @@
     coeff_beside = flip(coeffs, 1, count)
     node = share + first
     node, coeffs = lax.optimization_barrier((node, coeffs))
-    early = 2 * (leaves // 3)
-    own, first_blocks = pl.pallas_call(
+    own, down = pl.pallas_call(
         own_kernel,
-        out_shape=(product, sds((early, near - 1, points, points), f32)),
-        in_specs=[VMEM] * 2 + [ANY],
+        out_shape=(product, sds(branch_blocks.shape[1:], f32)),
+        in_specs=[VMEM] * 4,
         out_specs=(VMEM, VMEM),
-        scratch_shapes=[pltpu.SemaphoreType.DMA],
         compiler_params=PARAMS,
         name="near_own",
-    )(vectors_in, own_blocks, *in_hbm(near_blocks))
+    )(vectors_in, own_blocks, branch_blocks, cluster_transfer)
 
     bit = 2
     while bit < members:
@@ -304,39 +304,51 @@
     nodes = node[None]
     vec_across = across_chips(vec_beside, count)
     while 2 * bit < count:
+        if 4 * bit == count:
+            nodes, own = lax.optimization_barrier((nodes, own))
         nodes = jnp.concatenate([nodes, flip(nodes, bit + 1, count)], axis=0)
         bit *= 2
-    nodes, own = lax.optimization_barrier((nodes, own))
+    weights = pl.pallas_call(
+        weights_kernel,
+        out_shape=sds((leaves, rank, 2 * coupling_blocks.shape[1] * rank), bf16),
+        in_specs=[VMEM],
+        out_specs=VMEM,
+        compiler_params=PARAMS,
+        name="coupling_weights",
+    )(coupling_blocks)
+    nodes, weights = lax.optimization_barrier((nodes, weights))
     far_nodes = flip(nodes, bit + 1, count)
 
-    partial, other_blocks = pl.pallas_call(
+    partial = pl.pallas_call(
         coupling_kernel,
-        out_shape=(product, sds((leaves - early, near - 1, points, points), f32)),
-        in_specs=[SMEM] + [VMEM] * 6 + [ANY],
-        out_specs=(VMEM, VMEM),
+        out_shape=product,
+        in_specs=[SMEM] + [VMEM] * 6,
+        out_specs=VMEM,
         scratch_shapes=[
             pltpu.VMEM((3 * leaves, 2 * nv, 2 * rank), bf16),
             pltpu.VMEM((leaves, nv, rank), f32),
-            pltpu.SemaphoreType.DMA,
         ],
         compiler_params=PARAMS,
         name="coupling",
     )(
-        coupling_index.T, coeffs, coeff_across, coeff_beside, basis_in, own, coupling_blocks,
-        *in_hbm(near_blocks),
+        coupling_index.T, coeffs, coeff_across, coeff_beside, basis_in, own, weights,
     )
 
     return pl.pallas_call(
         last_kernel,
         out_shape=product,
-        in_specs=[SMEM] * 2 + [VMEM] * 11,
-        out_specs=VMEM,
-        scratch_shapes=[pltpu.VMEM((3 * leaves, 2 * nv, 2 * points), bf16)],
+        in_specs=[SMEM] * 2 + [VMEM] * 9,
+        out_specs=ANY,
+        scratch_shapes=[
+            pltpu.VMEM((3 * leaves, 2 * nv, 2 * points), bf16),
+            pltpu.VMEM((leaves, nv, points), f32),
+            pltpu.SemaphoreType.DMA((3,)),
+        ],
         compiler_params=PARAMS,
         name="last",
     )(
-        near_index.T, branch_index, vectors_in, vec_across, vec_beside, nodes, far_nodes, branch_blocks,
-        cluster_transfer, folded, partial, first_blocks, other_blocks,
+        near_index.T, branch_index, vectors_in, vec_across, vec_beside, nodes, far_nodes, down,
+        folded, partial, near_blocks,
     )
 
 

time: 25.1 us -> 24.4 us (0.972)
  Pallas kernels: 10.6 us -> 10.1 us
  starting transfers between devices: 10 us -> 9.73 us
    pallas_call x2 -> x3, Pallas kernels: 4.03 us -> 3.48 us  [the longest x1 1.83 us: per_device(): pl.pallas_call(coupling_kernel, out_shape=product, in_specs=[SMEM] + [VME...]
    ppermute x7, starting transfers between devices: 8.29 us -> 7.93 us  [flip(): return lax.ppermute(x, AXES, [(i, i ^ mask) for i in range(count)])]
  transfers between devices with their start and end apart: 9 -> 9, of which waited for: 4 -> 4; matrix products, arithmetic and copies ran while one was open for 0% -> 0% of each run, Pallas kernels for 30% -> 29%
where the time goes in v3:
time: 24.4 us; the launch traced here: 24.2 us
  Pallas kernels  10.1 us (41%)
  starting transfers between devices  9.73 us (40%)
  waiting for transfers between devices  4.27 us (18%)
    ppermute x7, starting transfers between devices, flip(): return lax.ppermute(x, AXES, [(i, i ^ mask) for i in range(count)])  7.93 us
    ppermute x7, waiting for transfers between devices, flip(): return lax.ppermute(x, AXES, [(i, i ^ mask) for i in range(count)])  4.26 us
    pallas_call x1, Pallas kernels, per_device(): pl.pallas_call(last_kernel, out_shape=product, in_specs=[SMEM] * 2 + [VME...  3.06 us
    pallas_call x1, Pallas kernels, per_device(): pl.pallas_call(up_kernel, out_shape=(sds((nv // 2, 2 * rank), f32), sds((...  3.04 us
    pallas_call x1, Pallas kernels, per_device(): pl.pallas_call(coupling_kernel, out_shape=product, in_specs=[SMEM] + [VME...  1.83 us
    ppermute x2, starting transfers between devices, across_chips(): return lax.ppermute(beside, AXES, pairs + [(count - 2, count - 1), (1, 0)])  1.8 us
    pallas_call x1, Pallas kernels, per_device(): pl.pallas_call(own_kernel, out_shape=(product, sds(branch_blocks.shape[1:...  0.9 us
    pallas_call x1, Pallas kernels, per_device(): pl.pallas_call(weights_kernel, out_shape=sds((leaves, rank, 2 * coupling_...  0.75 us
  transfers between devices with their start and end apart: 9, of which 4 were waited for; matrix products, arithmetic and copies ran while one was open for 0% of the time, Pallas kernels for 29%

profile of v3, /device:TPU:0, one launch (start us, length us, event | category | flops | bytes accessed | tf_op | source)
XLA Modules:
  0.0 24.2 jit_solution(16363771059086773916)
XLA Ops:
  0.0 0.0 copy-start.1
  0.0 0.0 copy-start.2
  0.0 0.5 %collective-permute-start = (f32[36,16,128]{2,1,0:T(8,128)}, f32[36,16,128]{2,1,0:T(8,128)S(1)}, u32[]{:S(2)}, u32[]{:S(2)}) collective-permute-start(f32[36,16,128]{2,1,0:T(8,128)} %vectors_hbm.1), channel_id=1, source_target_pairs={{0,1},{1,0},{2,3},{3,2},{4,5},{5,4},{6,7},{7,6},{8,9},{9,8},{10,11... | collective-permute-start | bytes 884744 | tf_op jit(solution)/shard_map/ppermute | solution.py:225
  0.5 0.0 copy-start
  0.5 3.0 %up.1 = (f32[8,128]{1,0:T(8,128)S(1)}, bf16[18,192,256]{2,1,0:T(8,128)(2,1)S(1)}, f32[36,16,128]{2,1,0:T(8,128)S(1)}, f32[36,64,128]{2,1,0:T(8,128)S(1)}, f32[36,128,128]{2,1,0:T(8,128)S(1)}) custom-call(f32[36,16,128]{2,1,0:T(8,128)} %vectors_hbm.1, f32[36,64,128]{2,1,0:T(8,128)} %basis_hbm.1, f32[36,64,64]{2,1,0:T(8,128)} %transfer_hbm.1, ...), custom_call_target="tpu_custom_call" | custom-call | tf_op jit(solution)/shard_map/up/pallas_call | solution.py:256
  3.5 0.1 collective-permute-start.2
  3.6 0.5 %coeffs.1 = f32[18,16,128]{2,1,0:T(8,128)S(1)} custom-call(f32[36,16,128]{2,1,0:T(8,128)S(1)} %get-tuple-element.18.vectors, f32[36,64,128]{2,1,0:T(8,128)S(1)} %get-tuple-element.20.basis), custom_call_target="tpu_custom_call" | custom-call | tf_op jit(solution)/shard_map/coeffs/pallas_call | solution.py:279
  4.1 0.6 %collective-permute-done.2 = f32[8,128]{1,0:T(8,128)S(1)} collective-permute-done((f32[8,128]{1,0:T(8,128)S(1)}, f32[8,128]{1,0:T(8,128)S(1)}, u32[]{:S(2)}, u32[]{:S(2)}) %collective-permute-start.2) | collective-permute-done | bytes 4128 | tf_op jit(solution)/shard_map/ppermute | solution.py:225
  4.7 2.6 %collective-permute-start.3 = (f32[8,128]{1,0:T(8,128)S(1)}, f32[8,128]{1,0:T(8,128)S(1)}, u32[]{:S(2)}, u32[]{:S(2)}) collective-permute-start(f32[8,128]{1,0:T(8,128)S(1)} %add.6), channel_id=1, source_target_pairs={{0,3},{1,2},{2,1},{3,0},{4,7},{5,6},{6,5},{7,4},{8,11},{9,10},{10,... | collective-permute-start | bytes 12296 | tf_op jit(solution)/shard_map/ppermute | solution.py:225
  7.4 0.2 collective-permute-start.7
  7.5 0.0 collective-permute-done.beside
  7.5 0.2 collective-permute-start.1
  7.8 0.9 %collective-permute-done.3 = f32[8,128]{1,0:T(8,128)S(1)} collective-permute-done((f32[8,128]{1,0:T(8,128)S(1)}, f32[8,128]{1,0:T(8,128)S(1)}, u32[]{:S(2)}, u32[]{:S(2)}) %collective-permute-start.3) | collective-permute-done | bytes 4128 | tf_op jit(solution)/shard_map/ppermute | solution.py:225
  8.7 1.7 %collective-permute-start.4 = (f32[1,8,128]{2,1,0:T(8,128)S(1)}, f32[1,8,128]{2,1,0:T(8,128)S(1)}, u32[]{:S(2)}, u32[]{:S(2)}) collective-permute-start(f32[1,8,128]{2,1,0:T(8,128)S(1)} %add_bitcast_fusion), channel_id=1, source_target_pairs={{0,5},{1,4},{2,7},{3,6},{4,1},{5,0},{6,3},{7,2},{8,13},{9,12},{10,... | collective-permute-start | bytes 12296 | tf_op jit(solution)/shard_map/ppermute | solution.py:225
  10.4 0.0 copy-done.1
  10.4 0.0 copy-done.2
  10.4 0.0 slice-start
  10.4 0.9 %near_own.1 = (f32[36,16,128]{2,1,0:T(8,128)S(1)}, f32[4,64,64]{2,1,0:T(8,128)S(1)}) custom-call(f32[36,16,128]{2,1,0:T(8,128)S(1)} %get-tuple-element.18.vectors, f32[36,128,128]{2,1,0:T(8,128)S(1)} %get-tuple-element.22.blocks, f32[1,4,64,64]{3,2,1,0:T(8,128)S(1)} %copy-done.2, f32[1,64,64]{2,1,0:T(8,128)S(1)} %copy-done.1), custom_call_target="tpu_custom_call" | custom-call | tf_op jit(solution)/shard_map/near_own/pallas_call | solution.py:290
  11.3 0.0 collective-permute-done.7.beside
  11.3 1.6 %collective-permute-start.8 = (f32[18,16,128]{2,1,0:T(8,128)S(1)}, f32[18,16,128]{2,1,0:T(8,128)S(1)}, u32[]{:S(2)}, u32[]{:S(2)}) collective-permute-start(f32[18,16,128]{2,1,0:T(8,128)S(1)} %collective-permute-done.7.beside), channel_id=1, source_target_pairs={{0,2},{2,4},{4,6},{6,8},{8,10},{10,12},{12,14},{14,16},{16,18},{18... | collective-permute-start | bytes 442376 | tf_op jit(solution)/shard_map/ppermute | solution.py:230
  12.9 0.6 %collective-permute-done.4 = f32[1,8,128]{2,1,0:T(8,128)S(1)} collective-permute-done((f32[1,8,128]{2,1,0:T(8,128)S(1)}, f32[1,8,128]{2,1,0:T(8,128)S(1)}, u32[]{:S(2)}, u32[]{:S(2)}) %collective-permute-start.4) | collective-permute-done | bytes 4128 | tf_op jit(solution)/shard_map/ppermute | solution.py:225
  13.5 0.0 copy-start.3
  13.5 0.0 slice-start.1
  13.5 0.4 %collective-permute-start.5 = (f32[2,8,128]{2,1,0:T(8,128)S(1)}, f32[2,8,128]{2,1,0:T(8,128)S(1)}, u32[]{:S(2)}, u32[]{:S(2)}) collective-permute-start(f32[2,8,128]{2,1,0:T(8,128)S(1)} %pad_maximum_fusion.1), channel_id=1, source_target_pairs={{0,9},{1,8},{2,11},{3,10},{4,13},{5,12},{6,15},{7,14},{8,1},{9,0},... | collective-permute-start | bytes 24584 | tf_op jit(solution)/shard_map/ppermute | solution.py:225
  13.9 0.0 copy-done
  13.9 0.7 %coupling_weights.1.blocks = bf16[36,64,512]{2,1,0:T(8,128)(2,1)S(1)} custom-call(f32[36,4,64,64]{3,2,1,0:T(8,128)S(1)} %copy-done), custom_call_target="tpu_custom_call" | custom-call | tf_op jit(solution)/shard_map/coupling_weights/pallas_call | solution.py:311
  14.7 0.0 copy-start.4
  14.7 0.0 copy-start.5
  14.7 2.1 %collective-permute-done.5 = f32[2,8,128]{2,1,0:T(8,128)S(1)} collective-permute-done((f32[2,8,128]{2,1,0:T(8,128)S(1)}, f32[2,8,128]{2,1,0:T(8,128)S(1)}, u32[]{:S(2)}, u32[]{:S(2)}) %collective-permute-start.5) | collective-permute-done | bytes 8224 | tf_op jit(solution)/shard_map/ppermute | solution.py:225
  16.8 2.5 %collective-permute-start.6 = (f32[4,8,128]{2,1,0:T(8,128)S(1)}, f32[4,8,128]{2,1,0:T(8,128)S(1)}, u32[]{:S(2)}, u32[]{:S(2)}) collective-permute-start(f32[4,8,128]{2,1,0:T(8,128)S(1)} %pad_maximum_fusion.nodes), channel_id=1, source_target_pairs={{0,17},{1,16},{2,19},{3,18},{4,21},{5,20},{6,23},{7,22},{8,25},{9,... | collective-permute-start | bytes 49160 | tf_op jit(solution)/shard_map/ppermute | solution.py:225
  19.2 0.0 collective-permute-done.8.across
  19.2 0.0 copy-done.3
  19.2 1.8 %coupling.1.partial = f32[36,16,128]{2,1,0:T(8,128)S(1)} custom-call(s32[4,36]{1,0:T(4,128)S(1)} %bitcast.6, f32[18,16,128]{2,1,0:T(8,128)S(1)} %coeffs.1, f32[18,16,128]{2,1,0:T(8,128)S(1)} %collective-permute-done.8.across, f32[18,16,128]{2,1,0:T(8,128)S(1)} %collective-permute-done.7.beside, f32[36,64,128]{2,1,0:T(8,128)S(1)} %get-tuple-element.20.basis, ...), custom_call_target="tpu_custom_call" | custom-call | tf_op jit(solution)/shard_map/coupling/pallas_call | solution.py:322
  21.1 0.0 collective-permute-done.6.far_nodes
  21.1 0.0 collective-permute-done.1.across
  21.1 0.0 slice-done
  21.1 0.0 slice-done.1
  21.1 0.0 copy-done.4
  21.1 0.0 copy-done.5
  21.2 3.1 %last.1 = f32[36,16,128]{2,1,0:T(8,128)} custom-call(s32[3,36]{1,0:T(4,128)S(1)} %bitcast.7, s32[1,4]{1,0:T(1,128)S(1)} %copy-done.5, f32[36,16,128]{2,1,0:T(8,128)S(1)} %get-tuple-element.18.vectors, f32[36,16,128]{2,1,0:T(8,128)S(1)} %collective-permute-done.1.across, f32[36,16,128]{2,1,0:T(8,128)S(1)} %collective-permute-done.beside, ...), custom_call_target="tpu_custom_call" | custom-call | tf_op jit(solution)/shard_map/last/pallas_call | solution.py:337
  (5 shorter events, 0.0 us)
Async XLA Ops:
  0.0 10.4 %copy-start.1 = (f32[1,64,64]{2,1,0:T(8,128)S(1)}, f32[1,64,64]{2,1,0:T(8,128)}, u32[]{:S(2)}) copy-start(f32[1,64,64]{2,1,0:T(8,128)} %top.1) | copy-start | bytes 49156
  0.0 10.4 %copy-start.2 = (f32[1,4,64,64]{3,2,1,0:T(8,128)S(1)}, f32[1,4,64,64]{3,2,1,0:T(8,128)}, u32[]{:S(2)}) copy-start(f32[1,4,64,64]{3,2,1,0:T(8,128)} %branch_blocks.1) | copy-start | bytes 196612
  0.0 7.5 %collective-permute-start = (f32[36,16,128]{2,1,0:T(8,128)}, f32[36,16,128]{2,1,0:T(8,128)S(1)}, u32[]{:S(2)}, u32[]{:S(2)}) collective-permute-start(f32[36,16,128]{2,1,0:T(8,128)} %vectors_hbm.1), channel_id=1, source_target_pairs={{0,1},{1,0},{2,3},{3,2},{4,5},{5,4},{6,7},{7,6},{8,9},{9,8},{10,11... | collective-permute-start | bytes 884744 | tf_op jit(solution)/shard_map/ppermute | solution.py:225
  0.5 13.5 %copy-start = (f32[36,4,64,64]{3,2,1,0:T(8,128)S(1)}, f32[36,4,64,64]{3,2,1,0:T(8,128)}, u32[]{:S(2)}) copy-start(f32[36,4,64,64]{3,2,1,0:T(8,128)} %blocks.2) | copy-start | bytes 7077892
  3.5 1.2 %collective-permute-start.2 = (f32[8,128]{1,0:T(8,128)S(1)}, f32[8,128]{1,0:T(8,128)S(1)}, u32[]{:S(2)}, u32[]{:S(2)}) collective-permute-start(f32[8,128]{1,0:T(8,128)S(1)} %get-tuple-element.19), channel_id=1, source_target_pairs={{0,1},{1,0},{2,3},{3,2},{4,5},{5,4},{6,7},{7,6},{8,9},{9,8},{10,11... | collective-permute-start | bytes 12296 | tf_op jit(solution)/shard_map/ppermute | solution.py:225
  4.7 4.0 %collective-permute-start.3 = (f32[8,128]{1,0:T(8,128)S(1)}, f32[8,128]{1,0:T(8,128)S(1)}, u32[]{:S(2)}, u32[]{:S(2)}) collective-permute-start(f32[8,128]{1,0:T(8,128)S(1)} %add.6), channel_id=1, source_target_pairs={{0,3},{1,2},{2,1},{3,0},{4,7},{5,6},{6,5},{7,4},{8,11},{9,10},{10,... | collective-permute-start | bytes 12296 | tf_op jit(solution)/shard_map/ppermute | solution.py:225
  7.4 3.9 %collective-permute-start.7 = (f32[18,16,128]{2,1,0:T(8,128)S(1)}, f32[18,16,128]{2,1,0:T(8,128)S(1)}, u32[]{:S(2)}, u32[]{:S(2)}) collective-permute-start(f32[18,16,128]{2,1,0:T(8,128)S(1)} %coeffs.1), channel_id=1, source_target_pairs={{0,1},{1,0},{2,3},{3,2},{4,5},{5,4},{6,7},{7,6},{8,9},{9,8},{10,11... | collective-permute-start | bytes 442376 | tf_op jit(solution)/shard_map/ppermute | solution.py:225
  7.5 13.6 %collective-permute-start.1 = (f32[36,16,128]{2,1,0:T(8,128)S(1)}, f32[36,16,128]{2,1,0:T(8,128)S(1)}, u32[]{:S(2)}, u32[]{:S(2)}) collective-permute-start(f32[36,16,128]{2,1,0:T(8,128)S(1)} %collective-permute-done.beside), channel_id=1, source_target_pairs={{0,2},{2,4},{4,6},{6,8},{8,10},{10,12},{12,14},{14,16},{16,18},{18... | collective-permute-start | bytes 884744 | tf_op jit(solution)/shard_map/ppermute | solution.py:230
  8.7 4.8 %collective-permute-start.4 = (f32[1,8,128]{2,1,0:T(8,128)S(1)}, f32[1,8,128]{2,1,0:T(8,128)S(1)}, u32[]{:S(2)}, u32[]{:S(2)}) collective-permute-start(f32[1,8,128]{2,1,0:T(8,128)S(1)} %add_bitcast_fusion), channel_id=1, source_target_pairs={{0,5},{1,4},{2,7},{3,6},{4,1},{5,0},{6,3},{7,2},{8,13},{9,12},{10,... | collective-permute-start | bytes 12296 | tf_op jit(solution)/shard_map/ppermute | solution.py:225
  10.4 10.7 %slice-start = ((s8[7077888]{0:T(1024)(128)(4,1)}), s8[4194304]{0:T(1024)(128)(4,1)S(1)}, s32[]{:S(2)}) async-start(s8[7077888]{0:T(1024)(128)(4,1)} %bitcast.4), calls=%async_computation | async-start | bytes 8388608
  11.3 7.9 %collective-permute-start.8 = (f32[18,16,128]{2,1,0:T(8,128)S(1)}, f32[18,16,128]{2,1,0:T(8,128)S(1)}, u32[]{:S(2)}, u32[]{:S(2)}) collective-permute-start(f32[18,16,128]{2,1,0:T(8,128)S(1)} %collective-permute-done.7.beside), channel_id=1, source_target_pairs={{0,2},{2,4},{4,6},{6,8},{8,10},{10,12},{12,14},{14,16},{16,18},{18... | collective-permute-start | bytes 442376 | tf_op jit(solution)/shard_map/ppermute | solution.py:230
  13.5 5.7 %copy-start.3 = (s32[36,4]{0,1:T(4,128)S(1)}, s32[36,4]{0,1:T(4,128)}, u32[]{:S(2)}) copy-start(s32[36,4]{0,1:T(4,128)} %param.14) | copy-start | bytes 1732
  13.5 7.6 %slice-start.1 = ((s8[7077888]{0:T(1024)(128)(4,1)}), s8[2883584]{0:T(1024)(128)(4,1)S(1)}, s32[]{:S(2)}) async-start(s8[7077888]{0:T(1024)(128)(4,1)} %bitcast.4), calls=%async_computation.1 | async-start | bytes 5767168
  13.5 3.2 %collective-permute-start.5 = (f32[2,8,128]{2,1,0:T(8,128)S(1)}, f32[2,8,128]{2,1,0:T(8,128)S(1)}, u32[]{:S(2)}, u32[]{:S(2)}) collective-permute-start(f32[2,8,128]{2,1,0:T(8,128)S(1)} %pad_maximum_fusion.1), channel_id=1, source_target_pairs={{0,9},{1,8},{2,11},{3,10},{4,13},{5,12},{6,15},{7,14},{8,1},{9,0},... | collective-permute-start | bytes 24584 | tf_op jit(solution)/shard_map/ppermute | solution.py:225
  14.7 6.5 %copy-start.4 = (s32[36,3]{0,1:T(4,128)S(1)}, s32[36,3]{0,1:T(4,128)}, u32[]{:S(2)}) copy-start(s32[36,3]{0,1:T(4,128)} %param.12) | copy-start | bytes 1300
  14.7 6.4 %copy-start.5 = (s32[1,4]{1,0:T(1,128)S(1)}, s32[1,4]{1,0:T(1,128)}, u32[]{:S(2)}) copy-start(s32[1,4]{1,0:T(1,128)} %branch_index.1) | copy-start | bytes 52
  16.8 4.3 %collective-permute-start.6 = (f32[4,8,128]{2,1,0:T(8,128)S(1)}, f32[4,8,128]{2,1,0:T(8,128)S(1)}, u32[]{:S(2)}, u32[]{:S(2)}) collective-permute-start(f32[4,8,128]{2,1,0:T(8,128)S(1)} %pad_maximum_fusion.nodes), channel_id=1, source_target_pairs={{0,17},{1,16},{2,19},{3,18},{4,21},{5,20},{6,23},{7,22},{8,25},{9,... | collective-permute-start | bytes 49160 | tf_op jit(solution)/shard_map/ppermute | solution.py:225

commit v4 on v3

--- a/solution.py
+++ b/solution.py
@@ -203,17 +203,20 @@
         for l in range(leaves):
             split[base + l] = rows_of(ref[l])
     anchor = first_leaf(leaves)
-    size, copies = leaves // sems.shape[0], []
-    for l in range(leaves):
-        if l % 2 == 0:
-            two = dot_nn(down, folded[l // 2])
-        rows = [split[near_index[k, l] - anchor] for k in range(1, near)]
-        others = turned_sum(rows, [blocks[l, k] for k in range(1, near)])
-        out[l] = partial[l] + others + two[:, (l % 2) * points : (l % 2 + 1) * points]
-        if (l + 1) % size == 0:
-            part = pl.ds(l + 1 - size, size)
-            copies.append(pltpu.make_async_copy(out.at[part], out_hbm.at[part], sems.at[l // size]))
-            copies[-1].start()
+    size, copies, lag = leaves // sems.shape[0], [], leaves // 3
+    for step in range(leaves + lag):
+        if step < leaves:
+            rows = [split[near_index[k, step] - anchor] for k in range(1, near)]
+            out[step] = partial[step] + turned_sum(rows, [blocks[step, k] for k in range(1, near)])
+        l = step - lag
+        if l >= 0:
+            if l % 2 == 0:
+                two = dot_nn(down, folded[l // 2])
+            out[l] = out[l] + two[:, (l % 2) * points : (l % 2 + 1) * points]
+            if (l + 1) % size == 0:
+                part = pl.ds(l + 1 - size, size)
+                copies.append(pltpu.make_async_copy(out.at[part], out_hbm.at[part], sems.at[l // size]))
+                copies[-1].start()
     wait_all(copies)
 
 

time: 24.4 us -> 24.3 us (level)
  no operation moved by 1% of the time
where the time goes in v4:
time: 24.3 us; the launch traced here: 24.2 us
  Pallas kernels  10 us (41%)
  starting transfers between devices  9.73 us (40%)
  waiting for transfers between devices  4.27 us (18%)
    ppermute x7, starting transfers between devices, flip(): return lax.ppermute(x, AXES, [(i, i ^ mask) for i in range(count)])  7.93 us
    ppermute x7, waiting for transfers between devices, flip(): return lax.ppermute(x, AXES, [(i, i ^ mask) for i in range(count)])  4.26 us
    pallas_call x1, Pallas kernels, per_device(): pl.pallas_call(up_kernel, out_shape=(sds((nv // 2, 2 * rank), f32), sds((...  3.04 us
    pallas_call x1, Pallas kernels, per_device(): pl.pallas_call(last_kernel, out_shape=product, in_specs=[SMEM] * 2 + [VME...  3 us
    pallas_call x1, Pallas kernels, per_device(): pl.pallas_call(coupling_kernel, out_shape=product, in_specs=[SMEM] + [VME...  1.83 us
    ppermute x2, starting transfers between devices, across_chips(): return lax.ppermute(beside, AXES, pairs + [(count - 2, count - 1), (1, 0)])  1.8 us
    pallas_call x1, Pallas kernels, per_device(): pl.pallas_call(own_kernel, out_shape=(product, sds(branch_blocks.shape[1:...  0.9 us
    pallas_call x1, Pallas kernels, per_device(): pl.pallas_call(weights_kernel, out_shape=sds((leaves, rank, 2 * coupling_...  0.75 us
  transfers between devices with their start and end apart: 9, of which 4 were waited for; matrix products, arithmetic and copies ran while one was open for 0% of the time, Pallas kernels for 29%

profile of v4, /device:TPU:0, one launch (start us, length us, event | category | flops | bytes accessed | tf_op | source)
XLA Modules:
  0.0 24.2 jit_solution(14217132276396214519)
XLA Ops:
  0.0 0.0 copy-start.1
  0.0 0.0 copy-start.2
  0.0 0.5 %collective-permute-start = (f32[36,16,128]{2,1,0:T(8,128)}, f32[36,16,128]{2,1,0:T(8,128)S(1)}, u32[]{:S(2)}, u32[]{:S(2)}) collective-permute-start(f32[36,16,128]{2,1,0:T(8,128)} %vectors_hbm.1), channel_id=1, source_target_pairs={{0,1},{1,0},{2,3},{3,2},{4,5},{5,4},{6,7},{7,6},{8,9},{9,8},{10,11... | collective-permute-start | bytes 884744 | tf_op jit(solution)/shard_map/ppermute | solution.py:228
  0.5 0.0 copy-start
  0.5 3.0 %up.1 = (f32[8,128]{1,0:T(8,128)S(1)}, bf16[18,192,256]{2,1,0:T(8,128)(2,1)S(1)}, f32[36,16,128]{2,1,0:T(8,128)S(1)}, f32[36,64,128]{2,1,0:T(8,128)S(1)}, f32[36,128,128]{2,1,0:T(8,128)S(1)}) custom-call(f32[36,16,128]{2,1,0:T(8,128)} %vectors_hbm.1, f32[36,64,128]{2,1,0:T(8,128)} %basis_hbm.1, f32[36,64,64]{2,1,0:T(8,128)} %transfer_hbm.1, ...), custom_call_target="tpu_custom_call" | custom-call | tf_op jit(solution)/shard_map/up/pallas_call | solution.py:259
  3.5 0.1 collective-permute-start.2
  3.6 0.5 %coeffs.1 = f32[18,16,128]{2,1,0:T(8,128)S(1)} custom-call(f32[36,16,128]{2,1,0:T(8,128)S(1)} %get-tuple-element.18.vectors, f32[36,64,128]{2,1,0:T(8,128)S(1)} %get-tuple-element.20.basis), custom_call_target="tpu_custom_call" | custom-call | tf_op jit(solution)/shard_map/coeffs/pallas_call | solution.py:282
  4.1 0.6 %collective-permute-done.2 = f32[8,128]{1,0:T(8,128)S(1)} collective-permute-done((f32[8,128]{1,0:T(8,128)S(1)}, f32[8,128]{1,0:T(8,128)S(1)}, u32[]{:S(2)}, u32[]{:S(2)}) %collective-permute-start.2) | collective-permute-done | bytes 4128 | tf_op jit(solution)/shard_map/ppermute | solution.py:228
  4.7 2.6 %collective-permute-start.3 = (f32[8,128]{1,0:T(8,128)S(1)}, f32[8,128]{1,0:T(8,128)S(1)}, u32[]{:S(2)}, u32[]{:S(2)}) collective-permute-start(f32[8,128]{1,0:T(8,128)S(1)} %add.6), channel_id=1, source_target_pairs={{0,3},{1,2},{2,1},{3,0},{4,7},{5,6},{6,5},{7,4},{8,11},{9,10},{10,... | collective-permute-start | bytes 12296 | tf_op jit(solution)/shard_map/ppermute | solution.py:228
  7.4 0.2 collective-permute-start.7
  7.5 0.0 collective-permute-done.beside
  7.5 0.2 collective-permute-start.1
  7.8 0.9 %collective-permute-done.3 = f32[8,128]{1,0:T(8,128)S(1)} collective-permute-done((f32[8,128]{1,0:T(8,128)S(1)}, f32[8,128]{1,0:T(8,128)S(1)}, u32[]{:S(2)}, u32[]{:S(2)}) %collective-permute-start.3) | collective-permute-done | bytes 4128 | tf_op jit(solution)/shard_map/ppermute | solution.py:228
  8.7 1.7 %collective-permute-start.4 = (f32[1,8,128]{2,1,0:T(8,128)S(1)}, f32[1,8,128]{2,1,0:T(8,128)S(1)}, u32[]{:S(2)}, u32[]{:S(2)}) collective-permute-start(f32[1,8,128]{2,1,0:T(8,128)S(1)} %add_bitcast_fusion), channel_id=1, source_target_pairs={{0,5},{1,4},{2,7},{3,6},{4,1},{5,0},{6,3},{7,2},{8,13},{9,12},{10,... | collective-permute-start | bytes 12296 | tf_op jit(solution)/shard_map/ppermute | solution.py:228
  10.4 0.0 copy-done.1
  10.4 0.0 copy-done.2
  10.4 0.0 slice-start
  10.4 0.9 %near_own.1 = (f32[36,16,128]{2,1,0:T(8,128)S(1)}, f32[4,64,64]{2,1,0:T(8,128)S(1)}) custom-call(f32[36,16,128]{2,1,0:T(8,128)S(1)} %get-tuple-element.18.vectors, f32[36,128,128]{2,1,0:T(8,128)S(1)} %get-tuple-element.22.blocks, f32[1,4,64,64]{3,2,1,0:T(8,128)S(1)} %copy-done.2, f32[1,64,64]{2,1,0:T(8,128)S(1)} %copy-done.1), custom_call_target="tpu_custom_call" | custom-call | tf_op jit(solution)/shard_map/near_own/pallas_call | solution.py:293
  11.3 0.0 collective-permute-done.7.beside
  11.3 1.6 %collective-permute-start.8 = (f32[18,16,128]{2,1,0:T(8,128)S(1)}, f32[18,16,128]{2,1,0:T(8,128)S(1)}, u32[]{:S(2)}, u32[]{:S(2)}) collective-permute-start(f32[18,16,128]{2,1,0:T(8,128)S(1)} %collective-permute-done.7.beside), channel_id=1, source_target_pairs={{0,2},{2,4},{4,6},{6,8},{8,10},{10,12},{12,14},{14,16},{16,18},{18... | collective-permute-start | bytes 442376 | tf_op jit(solution)/shard_map/ppermute | solution.py:233
  12.9 0.6 %collective-permute-done.4 = f32[1,8,128]{2,1,0:T(8,128)S(1)} collective-permute-done((f32[1,8,128]{2,1,0:T(8,128)S(1)}, f32[1,8,128]{2,1,0:T(8,128)S(1)}, u32[]{:S(2)}, u32[]{:S(2)}) %collective-permute-start.4) | collective-permute-done | bytes 4128 | tf_op jit(solution)/shard_map/ppermute | solution.py:228
  13.5 0.0 copy-start.3
  13.5 0.0 slice-start.1
  13.5 0.4 %collective-permute-start.5 = (f32[2,8,128]{2,1,0:T(8,128)S(1)}, f32[2,8,128]{2,1,0:T(8,128)S(1)}, u32[]{:S(2)}, u32[]{:S(2)}) collective-permute-start(f32[2,8,128]{2,1,0:T(8,128)S(1)} %pad_maximum_fusion.1), channel_id=1, source_target_pairs={{0,9},{1,8},{2,11},{3,10},{4,13},{5,12},{6,15},{7,14},{8,1},{9,0},... | collective-permute-start | bytes 24584 | tf_op jit(solution)/shard_map/ppermute | solution.py:228
  13.9 0.0 copy-done
  13.9 0.7 %coupling_weights.1.blocks = bf16[36,64,512]{2,1,0:T(8,128)(2,1)S(1)} custom-call(f32[36,4,64,64]{3,2,1,0:T(8,128)S(1)} %copy-done), custom_call_target="tpu_custom_call" | custom-call | tf_op jit(solution)/shard_map/coupling_weights/pallas_call | solution.py:314
  14.7 0.0 copy-start.4
  14.7 0.0 copy-start.5
  14.7 2.1 %collective-permute-done.5 = f32[2,8,128]{2,1,0:T(8,128)S(1)} collective-permute-done((f32[2,8,128]{2,1,0:T(8,128)S(1)}, f32[2,8,128]{2,1,0:T(8,128)S(1)}, u32[]{:S(2)}, u32[]{:S(2)}) %collective-permute-start.5) | collective-permute-done | bytes 8224 | tf_op jit(solution)/shard_map/ppermute | solution.py:228
  16.8 2.5 %collective-permute-start.6 = (f32[4,8,128]{2,1,0:T(8,128)S(1)}, f32[4,8,128]{2,1,0:T(8,128)S(1)}, u32[]{:S(2)}, u32[]{:S(2)}) collective-permute-start(f32[4,8,128]{2,1,0:T(8,128)S(1)} %pad_maximum_fusion.nodes), channel_id=1, source_target_pairs={{0,17},{1,16},{2,19},{3,18},{4,21},{5,20},{6,23},{7,22},{8,25},{9,... | collective-permute-start | bytes 49160 | tf_op jit(solution)/shard_map/ppermute | solution.py:228
  19.2 0.0 collective-permute-done.8.across
  19.2 0.0 copy-done.3
  19.2 1.8 %coupling.1.partial = f32[36,16,128]{2,1,0:T(8,128)S(1)} custom-call(s32[4,36]{1,0:T(4,128)S(1)} %bitcast.6, f32[18,16,128]{2,1,0:T(8,128)S(1)} %coeffs.1, f32[18,16,128]{2,1,0:T(8,128)S(1)} %collective-permute-done.8.across, f32[18,16,128]{2,1,0:T(8,128)S(1)} %collective-permute-done.7.beside, f32[36,64,128]{2,1,0:T(8,128)S(1)} %get-tuple-element.20.basis, ...), custom_call_target="tpu_custom_call" | custom-call | tf_op jit(solution)/shard_map/coupling/pallas_call | solution.py:325
  21.1 0.0 collective-permute-done.6.far_nodes
  21.1 0.0 collective-permute-done.1.across
  21.1 0.0 slice-done
  21.1 0.0 slice-done.1
  21.1 0.0 copy-done.4
  21.1 0.0 copy-done.5
  21.2 3.0 %last.1 = f32[36,16,128]{2,1,0:T(8,128)} custom-call(s32[3,36]{1,0:T(4,128)S(1)} %bitcast.7, s32[1,4]{1,0:T(1,128)S(1)} %copy-done.5, f32[36,16,128]{2,1,0:T(8,128)S(1)} %get-tuple-element.18.vectors, f32[36,16,128]{2,1,0:T(8,128)S(1)} %collective-permute-done.1.across, f32[36,16,128]{2,1,0:T(8,128)S(1)} %collective-permute-done.beside, ...), custom_call_target="tpu_custom_call" | custom-call | tf_op jit(solution)/shard_map/last/pallas_call | solution.py:340
  (5 shorter events, 0.0 us)
Async XLA Ops:
  0.0 10.4 %copy-start.1 = (f32[1,64,64]{2,1,0:T(8,128)S(1)}, f32[1,64,64]{2,1,0:T(8,128)}, u32[]{:S(2)}) copy-start(f32[1,64,64]{2,1,0:T(8,128)} %top.1) | copy-start | bytes 49156
  0.0 10.4 %copy-start.2 = (f32[1,4,64,64]{3,2,1,0:T(8,128)S(1)}, f32[1,4,64,64]{3,2,1,0:T(8,128)}, u32[]{:S(2)}) copy-start(f32[1,4,64,64]{3,2,1,0:T(8,128)} %branch_blocks.1) | copy-start | bytes 196612
  0.0 7.5 %collective-permute-start = (f32[36,16,128]{2,1,0:T(8,128)}, f32[36,16,128]{2,1,0:T(8,128)S(1)}, u32[]{:S(2)}, u32[]{:S(2)}) collective-permute-start(f32[36,16,128]{2,1,0:T(8,128)} %vectors_hbm.1), channel_id=1, source_target_pairs={{0,1},{1,0},{2,3},{3,2},{4,5},{5,4},{6,7},{7,6},{8,9},{9,8},{10,11... | collective-permute-start | bytes 884744 | tf_op jit(solution)/shard_map/ppermute | solution.py:228
  0.5 13.5 %copy-start = (f32[36,4,64,64]{3,2,1,0:T(8,128)S(1)}, f32[36,4,64,64]{3,2,1,0:T(8,128)}, u32[]{:S(2)}) copy-start(f32[36,4,64,64]{3,2,1,0:T(8,128)} %blocks.2) | copy-start | bytes 7077892
  3.5 1.2 %collective-permute-start.2 = (f32[8,128]{1,0:T(8,128)S(1)}, f32[8,128]{1,0:T(8,128)S(1)}, u32[]{:S(2)}, u32[]{:S(2)}) collective-permute-start(f32[8,128]{1,0:T(8,128)S(1)} %get-tuple-element.19), channel_id=1, source_target_pairs={{0,1},{1,0},{2,3},{3,2},{4,5},{5,4},{6,7},{7,6},{8,9},{9,8},{10,11... | collective-permute-start | bytes 12296 | tf_op jit(solution)/shard_map/ppermute | solution.py:228
  4.7 4.0 %collective-permute-start.3 = (f32[8,128]{1,0:T(8,128)S(1)}, f32[8,128]{1,0:T(8,128)S(1)}, u32[]{:S(2)}, u32[]{:S(2)}) collective-permute-start(f32[8,128]{1,0:T(8,128)S(1)} %add.6), channel_id=1, source_target_pairs={{0,3},{1,2},{2,1},{3,0},{4,7},{5,6},{6,5},{7,4},{8,11},{9,10},{10,... | collective-permute-start | bytes 12296 | tf_op jit(solution)/shard_map/ppermute | solution.py:228
  7.4 3.9 %collective-permute-start.7 = (f32[18,16,128]{2,1,0:T(8,128)S(1)}, f32[18,16,128]{2,1,0:T(8,128)S(1)}, u32[]{:S(2)}, u32[]{:S(2)}) collective-permute-start(f32[18,16,128]{2,1,0:T(8,128)S(1)} %coeffs.1), channel_id=1, source_target_pairs={{0,1},{1,0},{2,3},{3,2},{4,5},{5,4},{6,7},{7,6},{8,9},{9,8},{10,11... | collective-permute-start | bytes 442376 | tf_op jit(solution)/shard_map/ppermute | solution.py:228
  7.5 13.6 %collective-permute-start.1 = (f32[36,16,128]{2,1,0:T(8,128)S(1)}, f32[36,16,128]{2,1,0:T(8,128)S(1)}, u32[]{:S(2)}, u32[]{:S(2)}) collective-permute-start(f32[36,16,128]{2,1,0:T(8,128)S(1)} %collective-permute-done.beside), channel_id=1, source_target_pairs={{0,2},{2,4},{4,6},{6,8},{8,10},{10,12},{12,14},{14,16},{16,18},{18... | collective-permute-start | bytes 884744 | tf_op jit(solution)/shard_map/ppermute | solution.py:233
  8.7 4.8 %collective-permute-start.4 = (f32[1,8,128]{2,1,0:T(8,128)S(1)}, f32[1,8,128]{2,1,0:T(8,128)S(1)}, u32[]{:S(2)}, u32[]{:S(2)}) collective-permute-start(f32[1,8,128]{2,1,0:T(8,128)S(1)} %add_bitcast_fusion), channel_id=1, source_target_pairs={{0,5},{1,4},{2,7},{3,6},{4,1},{5,0},{6,3},{7,2},{8,13},{9,12},{10,... | collective-permute-start | bytes 12296 | tf_op jit(solution)/shard_map/ppermute | solution.py:228
  10.4 10.7 %slice-start = ((s8[7077888]{0:T(1024)(128)(4,1)}), s8[4194304]{0:T(1024)(128)(4,1)S(1)}, s32[]{:S(2)}) async-start(s8[7077888]{0:T(1024)(128)(4,1)} %bitcast.4), calls=%async_computation | async-start | bytes 8388608
  11.3 7.9 %collective-permute-start.8 = (f32[18,16,128]{2,1,0:T(8,128)S(1)}, f32[18,16,128]{2,1,0:T(8,128)S(1)}, u32[]{:S(2)}, u32[]{:S(2)}) collective-permute-start(f32[18,16,128]{2,1,0:T(8,128)S(1)} %collective-permute-done.7.beside), channel_id=1, source_target_pairs={{0,2},{2,4},{4,6},{6,8},{8,10},{10,12},{12,14},{14,16},{16,18},{18... | collective-permute-start | bytes 442376 | tf_op jit(solution)/shard_map/ppermute | solution.py:233
  13.5 5.7 %copy-start.3 = (s32[36,4]{0,1:T(4,128)S(1)}, s32[36,4]{0,1:T(4,128)}, u32[]{:S(2)}) copy-start(s32[36,4]{0,1:T(4,128)} %param.14) | copy-start | bytes 1732
  13.5 7.6 %slice-start.1 = ((s8[7077888]{0:T(1024)(128)(4,1)}), s8[2883584]{0:T(1024)(128)(4,1)S(1)}, s32[]{:S(2)}) async-start(s8[7077888]{0:T(1024)(128)(4,1)} %bitcast.4), calls=%async_computation.1 | async-start | bytes 5767168
  13.5 3.2 %collective-permute-start.5 = (f32[2,8,128]{2,1,0:T(8,128)S(1)}, f32[2,8,128]{2,1,0:T(8,128)S(1)}, u32[]{:S(2)}, u32[]{:S(2)}) collective-permute-start(f32[2,8,128]{2,1,0:T(8,128)S(1)} %pad_maximum_fusion.1), channel_id=1, source_target_pairs={{0,9},{1,8},{2,11},{3,10},{4,13},{5,12},{6,15},{7,14},{8,1},{9,0},... | collective-permute-start | bytes 24584 | tf_op jit(solution)/shard_map/ppermute | solution.py:228
  14.7 6.5 %copy-start.4 = (s32[36,3]{0,1:T(4,128)S(1)}, s32[36,3]{0,1:T(4,128)}, u32[]{:S(2)}) copy-start(s32[36,3]{0,1:T(4,128)} %param.12) | copy-start | bytes 1300
  14.7 6.4 %copy-start.5 = (s32[1,4]{1,0:T(1,128)S(1)}, s32[1,4]{1,0:T(1,128)}, u32[]{:S(2)}) copy-start(s32[1,4]{1,0:T(1,128)} %branch_index.1) | copy-start | bytes 52
  16.8 4.3 %collective-permute-start.6 = (f32[4,8,128]{2,1,0:T(8,128)S(1)}, f32[4,8,128]{2,1,0:T(8,128)S(1)}, u32[]{:S(2)}, u32[]{:S(2)}) collective-permute-start(f32[4,8,128]{2,1,0:T(8,128)S(1)} %pad_maximum_fusion.nodes), channel_id=1, source_target_pairs={{0,17},{1,16},{2,19},{3,18},{4,21},{5,20},{6,23},{7,22},{8,25},{9,... | collective-permute-start | bytes 49160 | tf_op jit(solution)/shard_map/ppermute | solution.py:228

commit v5 on v4

--- a/solution.py
+++ b/solution.py
@@ -154,15 +154,16 @@
         out[l] = turned_sum([rows_of(vectors[l])], [blocks[l]])
 
 
-def weights_kernel(blocks, out):
+def weights_kernel(blocks, basis, out, basis_out):
     for l in range(blocks.shape[0]):
+        basis_out[l] = weights_of(basis[l], 0)
         out[l] = jnp.concatenate([weights_of(blocks[l, k], 1) for k in range(blocks.shape[1])], axis=1)
 
 
 def coupling_kernel(
     index, coeffs, across, beside, basis, near, blocks, out, split, far
 ):
-    leaves, (coup, rank) = basis.shape[0], (index.shape[0], basis.shape[1])
+    leaves, coup, rank, nv = basis.shape[0], index.shape[0], basis.shape[1] // 2, out.shape[1]
     @then
     def _():
         half = leaves // 2
@@ -181,7 +182,9 @@
             weights = blocks[l]
             far[l] = both(dot_nt(rows, weights))
         for l in range(leaves):
-            out[l] = near[l] + three(dot_nn, far[l], basis[l])
+            rows = jnp.concatenate(halves(far[l]), axis=0)
+            wide = dot_nn(rows, basis[l, :rank])
+            out[l] = near[l] + wide[:nv] + wide[nv:] + dot_nn(rows[:nv], basis[l, rank:])
 
 def last_kernel(
     near_index, branch_index, vectors, across, beside, nodes, far_nodes, steps, folded, partial, blocks,
@@ -311,14 +314,17 @@
             nodes, own = lax.optimization_barrier((nodes, own))
         nodes = jnp.concatenate([nodes, flip(nodes, bit + 1, count)], axis=0)
         bit *= 2
-    weights = pl.pallas_call(
+    weights, basis_parts = pl.pallas_call(
         weights_kernel,
-        out_shape=sds((leaves, rank, 2 * coupling_blocks.shape[1] * rank), bf16),
-        in_specs=[VMEM],
-        out_specs=VMEM,
+        out_shape=(
+            sds((leaves, rank, 2 * coupling_blocks.shape[1] * rank), bf16),
+            sds((leaves, 2 * rank, points), bf16),
+        ),
+        in_specs=[VMEM] * 2,
+        out_specs=(VMEM, VMEM),
         compiler_params=PARAMS,
         name="coupling_weights",
-    )(coupling_blocks)
+    )(coupling_blocks, basis_in)
     nodes, weights = lax.optimization_barrier((nodes, weights))
     far_nodes = flip(nodes, bit + 1, count)
 
@@ -334,7 +340,7 @@
         compiler_params=PARAMS,
         name="coupling",
     )(
-        coupling_index.T, coeffs, coeff_across, coeff_beside, basis_in, own, weights,
+        coupling_index.T, coeffs, coeff_across, coeff_beside, basis_parts, own, weights,
     )
 
     return pl.pallas_call(

time: 24.3 us -> 24.3 us (level)
  no operation moved by 1% of the time
where the time goes in v5:
time: 24.3 us; the launch traced here: 24.2 us
  Pallas kernels  10.1 us (42%)
  starting transfers between devices  9.73 us (40%)
  waiting for transfers between devices  4.22 us (17%)
    ppermute x7, starting transfers between devices, flip(): return lax.ppermute(x, AXES, [(i, i ^ mask) for i in range(count)])  7.93 us
    ppermute x7, waiting for transfers between devices, flip(): return lax.ppermute(x, AXES, [(i, i ^ mask) for i in range(count)])  4.22 us
    pallas_call x1, Pallas kernels, per_device(): pl.pallas_call(up_kernel, out_shape=(sds((nv // 2, 2 * rank), f32), sds((...  3.05 us
    pallas_call x1, Pallas kernels, per_device(): pl.pallas_call(last_kernel, out_shape=product, in_specs=[SMEM] * 2 + [VME...  3.02 us
    pallas_call x1, Pallas kernels, per_device(): pl.pallas_call(coupling_kernel, out_shape=product, in_specs=[SMEM] + [VME...  1.84 us
    ppermute x2, starting transfers between devices, across_chips(): return lax.ppermute(beside, AXES, pairs + [(count - 2, count - 1), (1, 0)])  1.8 us
    pallas_call x1, Pallas kernels, per_device(): pl.pallas_call(own_kernel, out_shape=(product, sds(branch_blocks.shape[1:...  0.9 us
    pallas_call x1, Pallas kernels, per_device(): pl.pallas_call(weights_kernel, out_shape=(sds((leaves, rank, 2 * coupling...  0.82 us
  transfers between devices with their start and end apart: 9, of which 4 were waited for; matrix products, arithmetic and copies ran while one was open for 0% of the time, Pallas kernels for 29%

profile of v5, /device:TPU:0, one launch (start us, length us, event | category | flops | bytes accessed | tf_op | source)
XLA Modules:
  0.0 24.2 jit_solution(4699215999012631470)
XLA Ops:
  0.0 0.0 copy-start.1
  0.0 0.0 copy-start.2
  0.0 0.5 %collective-permute-start = (f32[36,16,128]{2,1,0:T(8,128)}, f32[36,16,128]{2,1,0:T(8,128)S(1)}, u32[]{:S(2)}, u32[]{:S(2)}) collective-permute-start(f32[36,16,128]{2,1,0:T(8,128)} %vectors_hbm.1), channel_id=1, source_target_pairs={{0,1},{1,0},{2,3},{3,2},{4,5},{5,4},{6,7},{7,6},{8,9},{9,8},{10,11... | collective-permute-start | bytes 884744 | tf_op jit(solution)/shard_map/ppermute | solution.py:231
  0.5 0.0 copy-start
  0.5 3.1 %up.1 = (f32[8,128]{1,0:T(8,128)S(1)}, bf16[18,192,256]{2,1,0:T(8,128)(2,1)S(1)}, f32[36,16,128]{2,1,0:T(8,128)S(1)}, f32[36,64,128]{2,1,0:T(8,128)S(1)}, f32[36,128,128]{2,1,0:T(8,128)S(1)}) custom-call(f32[36,16,128]{2,1,0:T(8,128)} %vectors_hbm.1, f32[36,64,128]{2,1,0:T(8,128)} %basis_hbm.1, f32[36,64,64]{2,1,0:T(8,128)} %transfer_hbm.1, ...), custom_call_target="tpu_custom_call" | custom-call | tf_op jit(solution)/shard_map/up/pallas_call | solution.py:262
  3.5 0.1 collective-permute-start.2
  3.6 0.5 %coeffs.1 = f32[18,16,128]{2,1,0:T(8,128)S(1)} custom-call(f32[36,16,128]{2,1,0:T(8,128)S(1)} %get-tuple-element.20.vectors, f32[36,64,128]{2,1,0:T(8,128)S(1)} %get-tuple-element.22.basis), custom_call_target="tpu_custom_call" | custom-call | tf_op jit(solution)/shard_map/coeffs/pallas_call | solution.py:285
  4.1 0.6 %collective-permute-done.2 = f32[8,128]{1,0:T(8,128)S(1)} collective-permute-done((f32[8,128]{1,0:T(8,128)S(1)}, f32[8,128]{1,0:T(8,128)S(1)}, u32[]{:S(2)}, u32[]{:S(2)}) %collective-permute-start.2) | collective-permute-done | bytes 4128 | tf_op jit(solution)/shard_map/ppermute | solution.py:231
  4.8 2.6 %collective-permute-start.3 = (f32[8,128]{1,0:T(8,128)S(1)}, f32[8,128]{1,0:T(8,128)S(1)}, u32[]{:S(2)}, u32[]{:S(2)}) collective-permute-start(f32[8,128]{1,0:T(8,128)S(1)} %add.6), channel_id=1, source_target_pairs={{0,3},{1,2},{2,1},{3,0},{4,7},{5,6},{6,5},{7,4},{8,11},{9,10},{10,... | collective-permute-start | bytes 12296 | tf_op jit(solution)/shard_map/ppermute | solution.py:231
  7.4 0.2 collective-permute-start.7
  7.6 0.0 collective-permute-done.beside
  7.6 0.2 collective-permute-start.1
  7.8 0.9 %collective-permute-done.3 = f32[8,128]{1,0:T(8,128)S(1)} collective-permute-done((f32[8,128]{1,0:T(8,128)S(1)}, f32[8,128]{1,0:T(8,128)S(1)}, u32[]{:S(2)}, u32[]{:S(2)}) %collective-permute-start.3) | collective-permute-done | bytes 4128 | tf_op jit(solution)/shard_map/ppermute | solution.py:231
  8.7 1.7 %collective-permute-start.4 = (f32[1,8,128]{2,1,0:T(8,128)S(1)}, f32[1,8,128]{2,1,0:T(8,128)S(1)}, u32[]{:S(2)}, u32[]{:S(2)}) collective-permute-start(f32[1,8,128]{2,1,0:T(8,128)S(1)} %add_bitcast_fusion), channel_id=1, source_target_pairs={{0,5},{1,4},{2,7},{3,6},{4,1},{5,0},{6,3},{7,2},{8,13},{9,12},{10,... | collective-permute-start | bytes 12296 | tf_op jit(solution)/shard_map/ppermute | solution.py:231
  10.4 0.0 copy-done.1
  10.4 0.0 copy-done.2
  10.4 0.0 slice-start
  10.4 0.9 %near_own.1 = (f32[36,16,128]{2,1,0:T(8,128)S(1)}, f32[4,64,64]{2,1,0:T(8,128)S(1)}) custom-call(f32[36,16,128]{2,1,0:T(8,128)S(1)} %get-tuple-element.20.vectors, f32[36,128,128]{2,1,0:T(8,128)S(1)} %get-tuple-element.24.blocks, f32[1,4,64,64]{3,2,1,0:T(8,128)S(1)} %copy-done.2, f32[1,64,64]{2,1,0:T(8,128)S(1)} %copy-done.1), custom_call_target="tpu_custom_call" | custom-call | tf_op jit(solution)/shard_map/near_own/pallas_call | solution.py:296
  11.3 0.0 collective-permute-done.7.beside
  11.3 1.6 %collective-permute-start.8 = (f32[18,16,128]{2,1,0:T(8,128)S(1)}, f32[18,16,128]{2,1,0:T(8,128)S(1)}, u32[]{:S(2)}, u32[]{:S(2)}) collective-permute-start(f32[18,16,128]{2,1,0:T(8,128)S(1)} %collective-permute-done.7.beside), channel_id=1, source_target_pairs={{0,2},{2,4},{4,6},{6,8},{8,10},{10,12},{12,14},{14,16},{16,18},{18... | collective-permute-start | bytes 442376 | tf_op jit(solution)/shard_map/ppermute | solution.py:236
  12.9 0.6 %collective-permute-done.4 = f32[1,8,128]{2,1,0:T(8,128)S(1)} collective-permute-done((f32[1,8,128]{2,1,0:T(8,128)S(1)}, f32[1,8,128]{2,1,0:T(8,128)S(1)}, u32[]{:S(2)}, u32[]{:S(2)}) %collective-permute-start.4) | collective-permute-done | bytes 4128 | tf_op jit(solution)/shard_map/ppermute | solution.py:231
  13.5 0.0 copy-start.3
  13.5 0.0 slice-start.1
  13.5 0.4 %collective-permute-start.5 = (f32[2,8,128]{2,1,0:T(8,128)S(1)}, f32[2,8,128]{2,1,0:T(8,128)S(1)}, u32[]{:S(2)}, u32[]{:S(2)}) collective-permute-start(f32[2,8,128]{2,1,0:T(8,128)S(1)} %pad_maximum_fusion.1), channel_id=1, source_target_pairs={{0,9},{1,8},{2,11},{3,10},{4,13},{5,12},{6,15},{7,14},{8,1},{9,0},... | collective-permute-start | bytes 24584 | tf_op jit(solution)/shard_map/ppermute | solution.py:231
  13.9 0.0 copy-done
  13.9 0.8 %coupling_weights.1 = (bf16[36,64,512]{2,1,0:T(8,128)(2,1)S(1)}, bf16[36,128,128]{2,1,0:T(8,128)(2,1)S(1)}) custom-call(f32[36,4,64,64]{3,2,1,0:T(8,128)S(1)} %copy-done, f32[36,64,128]{2,1,0:T(8,128)S(1)} %get-tuple-element.22.basis), custom_call_target="tpu_custom_call" | custom-call | tf_op jit(solution)/shard_map/coupling_weights/pallas_call | solution.py:317
  14.8 2.0 %collective-permute-done.5 = f32[2,8,128]{2,1,0:T(8,128)S(1)} collective-permute-done((f32[2,8,128]{2,1,0:T(8,128)S(1)}, f32[2,8,128]{2,1,0:T(8,128)S(1)}, u32[]{:S(2)}, u32[]{:S(2)}) %collective-permute-start.5) | collective-permute-done | bytes 8224 | tf_op jit(solution)/shard_map/ppermute | solution.py:231
  16.8 2.5 %collective-permute-start.6 = (f32[4,8,128]{2,1,0:T(8,128)S(1)}, f32[4,8,128]{2,1,0:T(8,128)S(1)}, u32[]{:S(2)}, u32[]{:S(2)}) collective-permute-start(f32[4,8,128]{2,1,0:T(8,128)S(1)} %pad_maximum_fusion.nodes), channel_id=1, source_target_pairs={{0,17},{1,16},{2,19},{3,18},{4,21},{5,20},{6,23},{7,22},{8,25},{9,... | collective-permute-start | bytes 49160 | tf_op jit(solution)/shard_map/ppermute | solution.py:231
  19.3 0.0 collective-permute-done.8.across
  19.3 0.0 copy-done.3
  19.3 0.0 copy-start.4
  19.3 0.0 copy-start.5
  19.3 1.8 %coupling.1.partial = f32[36,16,128]{2,1,0:T(8,128)S(1)} custom-call(s32[4,36]{1,0:T(4,128)S(1)} %bitcast.6, f32[18,16,128]{2,1,0:T(8,128)S(1)} %coeffs.1, f32[18,16,128]{2,1,0:T(8,128)S(1)} %collective-permute-done.8.across, f32[18,16,128]{2,1,0:T(8,128)S(1)} %collective-permute-done.7.beside, bf16[36,128,128]{2,1,0:T(8,128)(2,1)S(1)} %get-tuple-element.32.basis, ...), custom_call_target="tpu_custom_call" | custom-call | tf_op jit(solution)/shard_map/coupling/pallas_call | solution.py:331
  21.1 0.0 collective-permute-done.6.far_nodes
  21.1 0.0 collective-permute-done.1.across
  21.1 0.0 slice-done
  21.1 0.0 slice-done.1
  21.2 0.0 copy-done.4
  21.2 0.0 copy-done.5
  21.2 3.0 %last.1 = f32[36,16,128]{2,1,0:T(8,128)} custom-call(s32[3,36]{1,0:T(4,128)S(1)} %bitcast.7, s32[1,4]{1,0:T(1,128)S(1)} %copy-done.5, f32[36,16,128]{2,1,0:T(8,128)S(1)} %get-tuple-element.20.vectors, f32[36,16,128]{2,1,0:T(8,128)S(1)} %collective-permute-done.1.across, f32[36,16,128]{2,1,0:T(8,128)S(1)} %collective-permute-done.beside, ...), custom_call_target="tpu_custom_call" | custom-call | tf_op jit(solution)/shard_map/last/pallas_call | solution.py:346
  (5 shorter events, 0.0 us)
Async XLA Ops:
  0.0 10.4 %copy-start.1 = (f32[1,64,64]{2,1,0:T(8,128)S(1)}, f32[1,64,64]{2,1,0:T(8,128)}, u32[]{:S(2)}) copy-start(f32[1,64,64]{2,1,0:T(8,128)} %top.1) | copy-start | bytes 49156
  0.0 10.4 %copy-start.2 = (f32[1,4,64,64]{3,2,1,0:T(8,128)S(1)}, f32[1,4,64,64]{3,2,1,0:T(8,128)}, u32[]{:S(2)}) copy-start(f32[1,4,64,64]{3,2,1,0:T(8,128)} %branch_blocks.1) | copy-start | bytes 196612
  0.0 7.6 %collective-permute-start = (f32[36,16,128]{2,1,0:T(8,128)}, f32[36,16,128]{2,1,0:T(8,128)S(1)}, u32[]{:S(2)}, u32[]{:S(2)}) collective-permute-start(f32[36,16,128]{2,1,0:T(8,128)} %vectors_hbm.1), channel_id=1, source_target_pairs={{0,1},{1,0},{2,3},{3,2},{4,5},{5,4},{6,7},{7,6},{8,9},{9,8},{10,11... | collective-permute-start | bytes 884744 | tf_op jit(solution)/shard_map/ppermute | solution.py:231
  0.5 13.5 %copy-start = (f32[36,4,64,64]{3,2,1,0:T(8,128)S(1)}, f32[36,4,64,64]{3,2,1,0:T(8,128)}, u32[]{:S(2)}) copy-start(f32[36,4,64,64]{3,2,1,0:T(8,128)} %blocks.2) | copy-start | bytes 7077892
  3.5 1.2 %collective-permute-start.2 = (f32[8,128]{1,0:T(8,128)S(1)}, f32[8,128]{1,0:T(8,128)S(1)}, u32[]{:S(2)}, u32[]{:S(2)}) collective-permute-start(f32[8,128]{1,0:T(8,128)S(1)} %get-tuple-element.21), channel_id=1, source_target_pairs={{0,1},{1,0},{2,3},{3,2},{4,5},{5,4},{6,7},{7,6},{8,9},{9,8},{10,11... | collective-permute-start | bytes 12296 | tf_op jit(solution)/shard_map/ppermute | solution.py:231
  4.8 4.0 %collective-permute-start.3 = (f32[8,128]{1,0:T(8,128)S(1)}, f32[8,128]{1,0:T(8,128)S(1)}, u32[]{:S(2)}, u32[]{:S(2)}) collective-permute-start(f32[8,128]{1,0:T(8,128)S(1)} %add.6), channel_id=1, source_target_pairs={{0,3},{1,2},{2,1},{3,0},{4,7},{5,6},{6,5},{7,4},{8,11},{9,10},{10,... | collective-permute-start | bytes 12296 | tf_op jit(solution)/shard_map/ppermute | solution.py:231
  7.4 3.9 %collective-permute-start.7 = (f32[18,16,128]{2,1,0:T(8,128)S(1)}, f32[18,16,128]{2,1,0:T(8,128)S(1)}, u32[]{:S(2)}, u32[]{:S(2)}) collective-permute-start(f32[18,16,128]{2,1,0:T(8,128)S(1)} %coeffs.1), channel_id=1, source_target_pairs={{0,1},{1,0},{2,3},{3,2},{4,5},{5,4},{6,7},{7,6},{8,9},{9,8},{10,11... | collective-permute-start | bytes 442376 | tf_op jit(solution)/shard_map/ppermute | solution.py:231
  7.6 13.6 %collective-permute-start.1 = (f32[36,16,128]{2,1,0:T(8,128)S(1)}, f32[36,16,128]{2,1,0:T(8,128)S(1)}, u32[]{:S(2)}, u32[]{:S(2)}) collective-permute-start(f32[36,16,128]{2,1,0:T(8,128)S(1)} %collective-permute-done.beside), channel_id=1, source_target_pairs={{0,2},{2,4},{4,6},{6,8},{8,10},{10,12},{12,14},{14,16},{16,18},{18... | collective-permute-start | bytes 884744 | tf_op jit(solution)/shard_map/ppermute | solution.py:236
  8.7 4.8 %collective-permute-start.4 = (f32[1,8,128]{2,1,0:T(8,128)S(1)}, f32[1,8,128]{2,1,0:T(8,128)S(1)}, u32[]{:S(2)}, u32[]{:S(2)}) collective-permute-start(f32[1,8,128]{2,1,0:T(8,128)S(1)} %add_bitcast_fusion), channel_id=1, source_target_pairs={{0,5},{1,4},{2,7},{3,6},{4,1},{5,0},{6,3},{7,2},{8,13},{9,12},{10,... | collective-permute-start | bytes 12296 | tf_op jit(solution)/shard_map/ppermute | solution.py:231
  10.4 10.7 %slice-start = ((s8[7077888]{0:T(1024)(128)(4,1)}), s8[4194304]{0:T(1024)(128)(4,1)S(1)}, s32[]{:S(2)}) async-start(s8[7077888]{0:T(1024)(128)(4,1)} %bitcast.4), calls=%async_computation | async-start | bytes 8388608
  11.3 7.9 %collective-permute-start.8 = (f32[18,16,128]{2,1,0:T(8,128)S(1)}, f32[18,16,128]{2,1,0:T(8,128)S(1)}, u32[]{:S(2)}, u32[]{:S(2)}) collective-permute-start(f32[18,16,128]{2,1,0:T(8,128)S(1)} %collective-permute-done.7.beside), channel_id=1, source_target_pairs={{0,2},{2,4},{4,6},{6,8},{8,10},{10,12},{12,14},{14,16},{16,18},{18... | collective-permute-start | bytes 442376 | tf_op jit(solution)/shard_map/ppermute | solution.py:236
  13.5 5.7 %copy-start.3 = (s32[36,4]{0,1:T(4,128)S(1)}, s32[36,4]{0,1:T(4,128)}, u32[]{:S(2)}) copy-start(s32[36,4]{0,1:T(4,128)} %param.14) | copy-start | bytes 1732
  13.5 7.6 %slice-start.1 = ((s8[7077888]{0:T(1024)(128)(4,1)}), s8[2883584]{0:T(1024)(128)(4,1)S(1)}, s32[]{:S(2)}) async-start(s8[7077888]{0:T(1024)(128)(4,1)} %bitcast.4), calls=%async_computation.1 | async-start | bytes 5767168
  13.5 3.2 %collective-permute-start.5 = (f32[2,8,128]{2,1,0:T(8,128)S(1)}, f32[2,8,128]{2,1,0:T(8,128)S(1)}, u32[]{:S(2)}, u32[]{:S(2)}) collective-permute-start(f32[2,8,128]{2,1,0:T(8,128)S(1)} %pad_maximum_fusion.1), channel_id=1, source_target_pairs={{0,9},{1,8},{2,11},{3,10},{4,13},{5,12},{6,15},{7,14},{8,1},{9,0},... | collective-permute-start | bytes 24584 | tf_op jit(solution)/shard_map/ppermute | solution.py:231
  16.8 4.3 %collective-permute-start.6 = (f32[4,8,128]{2,1,0:T(8,128)S(1)}, f32[4,8,128]{2,1,0:T(8,128)S(1)}, u32[]{:S(2)}, u32[]{:S(2)}) collective-permute-start(f32[4,8,128]{2,1,0:T(8,128)S(1)} %pad_maximum_fusion.nodes), channel_id=1, source_target_pairs={{0,17},{1,16},{2,19},{3,18},{4,21},{5,20},{6,23},{7,22},{8,25},{9,... | collective-permute-start | bytes 49160 | tf_op jit(solution)/shard_map/ppermute | solution.py:231
  19.3 1.9 %copy-start.4 = (s32[36,3]{0,1:T(4,128)S(1)}, s32[36,3]{0,1:T(4,128)}, u32[]{:S(2)}) copy-start(s32[36,3]{0,1:T(4,128)} %param.12) | copy-start | bytes 1300
  19.3 1.9 %copy-start.5 = (s32[1,4]{1,0:T(1,128)S(1)}, s32[1,4]{1,0:T(1,128)}, u32[]{:S(2)}) copy-start(s32[1,4]{1,0:T(1,128)} %branch_index.1) | copy-start | bytes 52
